TPU v7x, 32 devices: a whole 2x2x4 slice. The times are simulated.
32 devices in a mesh: dp: 4 (over y, x), fsdp: 8 (over z, core).
Axes of the slice: x: 2, y: 2, z: 4, core: 2. Of those that a mesh axis runs over, the one named last changes fastest.
Arguments:
- tok_ids: int32 [32, 128], P(('dp', 'fsdp')), may hold values from 0 to 50303
- targets: int32 [32, 128], P(('dp', 'fsdp')), may hold values from 0 to 50303
- loss_mask: int32 [32, 128], P(('dp', 'fsdp')), may hold values 0 or 1
- embed: float32 [50304, 768], P('fsdp'), may hold values from -0.4375 to 0.4375
- embed_m: float32 [50304, 768], P('fsdp'), may hold values from -7.6293945e-06 to 7.6293945e-06
- embed_v: float32 [50304, 768], P('fsdp'), may hold values from 2.1455721e-12 to 8.5822885e-12
- posit: float32 [1024, 768], P('fsdp'), may hold values from -3 to 3
- posit_m: float32 [1024, 768], P('fsdp'), may hold values from -7.6293945e-06 to 7.6293945e-06
- posit_v: float32 [1024, 768], P('fsdp'), may hold values from 2.1455721e-12 to 8.5822885e-12
- attn_in: float32 [768, 2304], P('fsdp'), may hold values from -0.21875 to 0.21875
- attn_in_m: float32 [768, 2304], P('fsdp'), may hold values from -7.6293945e-06 to 7.6293945e-06
- attn_in_v: float32 [768, 2304], P('fsdp'), may hold values from 2.1455721e-12 to 8.5822885e-12
- attn_out: float32 [768, 768], P('fsdp'), may hold values from -1.25 to 1.25
- attn_out_m: float32 [768, 768], P('fsdp'), may hold values from -7.6293945e-06 to 7.6293945e-06
- attn_out_v: float32 [768, 768], P('fsdp'), may hold values from 2.1455721e-12 to 8.5822885e-12
- mlp_in: float32 [768, 3072], P('fsdp'), may hold values from -0.21875 to 0.21875
- mlp_in_m: float32 [768, 3072], P('fsdp'), may hold values from -7.6293945e-06 to 7.6293945e-06
- mlp_in_v: float32 [768, 3072], P('fsdp'), may hold values from 2.1455721e-12 to 8.5822885e-12
- mlp_out: float32 [3072, 768], P('fsdp'), may hold values from -0.109375 to 0.109375
- mlp_out_m: float32 [3072, 768], P('fsdp'), may hold values from -7.6293945e-06 to 7.6293945e-06
- mlp_out_v: float32 [3072, 768], P('fsdp'), may hold values from 2.1455721e-12 to 8.5822885e-12
- small: float32 [109824], P('fsdp'), may hold values from -1 to 1.4
- small_m: float32 [109824], P('fsdp'), may hold values from -2.670288e-05 to 2.670288e-05
- small_v: float32 [109824], P('fsdp'), may hold values from 1.9310149e-11 to 7.7240596e-11
Outputs:
- loss: float32 [], replicated
- grad_norm: float32 [], replicated
- embed_new: float32 [50304, 768], P('fsdp')
- embed_m_new: float32 [50304, 768], P('fsdp')
- embed_v_new: float32 [50304, 768], P('fsdp')
- posit_new: float32 [1024, 768], P('fsdp')
- posit_m_new: float32 [1024, 768], P('fsdp')
- posit_v_new: float32 [1024, 768], P('fsdp')
- attn_in_new: float32 [768, 2304], P('fsdp')
- attn_in_m_new: float32 [768, 2304], P('fsdp')
- attn_in_v_new: float32 [768, 2304], P('fsdp')
- attn_out_new: float32 [768, 768], P('fsdp')
- attn_out_m_new: float32 [768, 768], P('fsdp')
- attn_out_v_new: float32 [768, 768], P('fsdp')
- mlp_in_new: float32 [768, 3072], P('fsdp')
- mlp_in_m_new: float32 [768, 3072], P('fsdp')
- mlp_in_v_new: float32 [768, 3072], P('fsdp')
- mlp_out_new: float32 [3072, 768], P('fsdp')
- mlp_out_m_new: float32 [3072, 768], P('fsdp')
- mlp_out_v_new: float32 [3072, 768], P('fsdp')
- small_new: float32 [109824], P('fsdp')
- small_m_new: float32 [109824], P('fsdp')
- small_v_new: float32 [109824], P('fsdp')
All inputs are finite; a program needn't handle non-finite values. No bound on the sum of `loss_mask` on one device may be relied on, other than what follows from the above.
Results may differ from a plain program's by a relative error of at most 0.01.
Values may be sent and summed in bfloat16 or wider, within the bound.
A program may use at most 384 MiB of HBM per device.

v0:
```python
from functools import reduce

import jax
import jax.numpy as jnp
from jax import lax
from jax.sharding import PartitionSpec as P

D = 768
H = 12
HD = 64
FF = 3072
STEP = 2


EPS = 1e-05
CLIP_LIMIT = 0.01
BETA = 0.5
DECAY = 0.1
ADAM_EPS = 1e-08


def combined_all(value, axis, join):
    pieces = jax.tree.map(lambda part: lax.all_gather(part, axis), value)
    head = jax.tree.map(lambda part: part[0], pieces)
    tail = jax.tree.map(lambda part: part[1:], pieces)
    subtotal, _ = lax.scan(lambda subtotal, piece: (join(subtotal, piece), None), head, tail)
    return subtotal


def dense(left, right):
    return jnp.dot(left, right, preferred_element_type=jnp.float32)


def dense_tn(left, right):
    return lax.dot_general(
        left, right, (((0,), (0,)), ((), ())), preferred_element_type=jnp.float32
    )


def dense_nt(left, right):
    return lax.dot_general(
        left, right, (((1,), (1,)), ((), ())), preferred_element_type=jnp.float32
    )


def layer_norm(values, gain, bias):
    center = values - jnp.mean(values, axis=-1, keepdims=True)
    spread = jnp.mean(center * center, axis=-1, keepdims=True)
    return center * lax.rsqrt(spread + EPS) * gain + bias


def features(inner):
    return jnp.concatenate(
        [jax.nn.softmax(inner, axis=-1), jax.nn.softmax(-inner, axis=-1)], axis=-1
    )


def gelu_tanh(values):
    return jax.nn.gelu(values, approximate=True)


def unpack(vector):
    cuts = [D, D, D, D, D, D, 3 * D, D, FF, D, H * HD * HD, H * HD * HD]
    pieces = []
    offset = 0
    for piece_len in cuts:
        pieces.append(vector[offset : offset + piece_len])
        offset = offset + piece_len
    return pieces


def rate_list():
    return (2.0 * D ** (-0.5), 0.5, D ** (-0.5), (32.0 / D) ** 0.5, D ** (-0.5), FF ** (-0.5), 0.1)


def norm_pull(values, gain, bias, cotangent):
    unused, pull = jax.vjp(layer_norm, values, gain, bias)
    return pull(cotangent)


def causal_mask(length):
    rows_idx = lax.broadcasted_iota(jnp.int32, (length, length), 0)
    cols_idx = lax.broadcasted_iota(jnp.int32, (length, length), 1)
    return (rows_idx >= cols_idx).astype(jnp.float32)


def layer_forward(inputs, mats, pieces):
    w_qkv, w_out, w_up, w_down = mats
    (
        gain_one,
        bias_one,
        gain_two,
        bias_two,
        gain_fin,
        bias_fin,
        bias_qkv,
        bias_out,
        bias_up,
        bias_down,
        map_query,
        map_key,
    ) = pieces
    length = inputs.shape[0]
    normed_one = layer_norm(inputs, gain_one, bias_one).astype(jnp.bfloat16)
    project = dense(normed_one, w_qkv) + bias_qkv
    queries = project[:, :D].astype(jnp.bfloat16).reshape(length, H, HD)
    keys_in = project[:, D : 2 * D].astype(jnp.bfloat16).reshape(length, H, HD)
    values_in = project[:, 2 * D :].astype(jnp.bfloat16).reshape(length, H, HD)
    maps_q = map_query.reshape(H, HD, HD).astype(jnp.bfloat16)
    maps_k = map_key.reshape(H, HD, HD).astype(jnp.bfloat16)
    inner_q = jnp.einsum("shd,hde->she", queries, maps_q, preferred_element_type=jnp.float32)
    inner_k = jnp.einsum("shd,hde->she", keys_in, maps_k, preferred_element_type=jnp.float32)
    feat_q = features(inner_q).astype(jnp.bfloat16)
    feat_k = features(inner_k).astype(jnp.bfloat16)
    scores = jnp.einsum(
        "thf,shf->hts", feat_q, feat_k, preferred_element_type=jnp.float32
    ) * causal_mask(length)
    totals = jnp.sum(scores, axis=-1)
    scores_low = scores.astype(jnp.bfloat16)
    numer = jnp.einsum("hts,shd->thd", scores_low, values_in, preferred_element_type=jnp.float32)
    attended = numer / jnp.transpose(totals)[:, :, None]
    att_low = attended.reshape(length, D).astype(jnp.bfloat16)
    resid_one = inputs + dense(att_low, w_out) + bias_out
    normed_two = layer_norm(resid_one, gain_two, bias_two).astype(jnp.bfloat16)
    pre_act = dense(normed_two, w_up) + bias_up
    act_low = gelu_tanh(pre_act).astype(jnp.bfloat16)
    resid_two = resid_one + dense(act_low, w_down) + bias_down
    final = layer_norm(resid_two, gain_fin, bias_fin)
    saved = (
        normed_one,
        queries,
        keys_in,
        values_in,
        maps_q,
        maps_k,
        inner_q,
        inner_k,
        feat_q,
        feat_k,
        scores_low,
        totals,
        numer,
        att_low,
        resid_one,
        normed_two,
        pre_act,
        act_low,
        resid_two,
    )
    return (final, saved)


def layer_backward(inputs, mats, pieces, saved, d_final):
    w_qkv, w_out, w_up, w_down = mats
    (
        gain_one,
        bias_one,
        gain_two,
        bias_two,
        gain_fin,
        bias_fin,
        bias_qkv,
        bias_out,
        bias_up,
        bias_down,
        map_query,
        map_key,
    ) = pieces
    (
        normed_one,
        queries,
        keys_in,
        values_in,
        maps_q,
        maps_k,
        inner_q,
        inner_k,
        feat_q,
        feat_k,
        scores_low,
        totals,
        numer,
        att_low,
        resid_one,
        normed_two,
        pre_act,
        act_low,
        resid_two,
    ) = saved
    length = inputs.shape[0]
    d_resid_two, d_gain_fin, d_bias_fin = norm_pull(resid_two, gain_fin, bias_fin, d_final)
    d_bias_down = jnp.sum(d_resid_two, axis=0)
    d_down_low = d_resid_two.astype(jnp.bfloat16)
    g_down = dense_tn(act_low, d_down_low)
    d_act = dense_nt(d_down_low, w_down)
    unused, gelu_back = jax.vjp(gelu_tanh, pre_act)
    d_pre = gelu_back(d_act)[0]
    d_bias_up = jnp.sum(d_pre, axis=0)
    d_pre_low = d_pre.astype(jnp.bfloat16)
    g_up = dense_tn(normed_two, d_pre_low)
    d_normed_two = dense_nt(d_pre_low, w_up)
    d_resid_part, d_gain_two, d_bias_two = norm_pull(resid_one, gain_two, bias_two, d_normed_two)
    d_resid_one = d_resid_two + d_resid_part
    d_bias_out = jnp.sum(d_resid_one, axis=0)
    d_out_low = d_resid_one.astype(jnp.bfloat16)
    g_out = dense_tn(att_low, d_out_low)
    d_attended = dense_nt(d_out_low, w_out).reshape(length, H, HD)
    inverse = 1.0 / jnp.transpose(totals)
    d_numer_low = (d_attended * inverse[:, :, None]).astype(jnp.bfloat16)
    d_totals = jnp.transpose(-jnp.sum(d_attended * numer, axis=-1) * inverse * inverse)
    d_scores = jnp.einsum(
        "thd,shd->hts", d_numer_low, values_in, preferred_element_type=jnp.float32
    )
    d_scores_low = ((d_scores + d_totals[:, :, None]) * causal_mask(length)).astype(jnp.bfloat16)
    d_values = jnp.einsum(
        "hts,thd->shd", scores_low, d_numer_low, preferred_element_type=jnp.float32
    )
    d_feat_q = jnp.einsum("hts,shf->thf", d_scores_low, feat_k, preferred_element_type=jnp.float32)
    d_feat_k = jnp.einsum("hts,thf->shf", d_scores_low, feat_q, preferred_element_type=jnp.float32)
    unused, pull_q = jax.vjp(features, inner_q)
    unused, pull_k = jax.vjp(features, inner_k)
    d_inner_q = pull_q(d_feat_q)[0].astype(jnp.bfloat16)
    d_inner_k = pull_k(d_feat_k)[0].astype(jnp.bfloat16)
    g_map_q = jnp.einsum("shd,she->hde", queries, d_inner_q, preferred_element_type=jnp.float32)
    g_map_k = jnp.einsum("shd,she->hde", keys_in, d_inner_k, preferred_element_type=jnp.float32)
    d_queries = jnp.einsum("she,hde->shd", d_inner_q, maps_q, preferred_element_type=jnp.float32)
    d_keys = jnp.einsum("she,hde->shd", d_inner_k, maps_k, preferred_element_type=jnp.float32)
    d_project = jnp.concatenate(
        [d_queries.reshape(length, D), d_keys.reshape(length, D), d_values.reshape(length, D)],
        axis=1,
    )
    d_bias_qkv = jnp.sum(d_project, axis=0)
    d_project_low = d_project.astype(jnp.bfloat16)
    g_qkv = dense_tn(normed_one, d_project_low)
    d_normed_one = dense_nt(d_project_low, w_qkv)
    d_input_part, d_gain_one, d_bias_one = norm_pull(inputs, gain_one, bias_one, d_normed_one)
    d_inputs = d_resid_one + d_input_part
    g_small = jnp.concatenate(
        [
            d_gain_one,
            d_bias_one,
            d_gain_two,
            d_bias_two,
            d_gain_fin,
            d_bias_fin,
            d_bias_qkv,
            d_bias_out,
            d_bias_up,
            d_bias_down,
            g_map_q.reshape(-1),
            g_map_k.reshape(-1),
        ]
    )
    return (d_inputs, (g_qkv, g_out, g_up, g_down), g_small)


def adam_update(weight, first_old, second_old, gradient, rate):
    first_new = BETA * first_old + (1.0 - BETA) * gradient
    second_new = BETA * second_old + (1.0 - BETA) * gradient * gradient
    bias_fix = 1.0 - BETA**STEP
    weight_new = weight - rate * (
        first_new / bias_fix / (jnp.sqrt(second_new / bias_fix) + ADAM_EPS) + DECAY * weight
    )
    return (weight_new, first_new, second_new)


def combine_lse(first_part, second_part):
    top = jnp.maximum(first_part[0], second_part[0])
    merged = first_part[1] * jnp.exp(first_part[0] - top) + second_part[1] * jnp.exp(
        second_part[0] - top
    )
    return (top, merged, first_part[2] + second_part[2])


def body(
    tok_ids,
    targets,
    loss_mask,
    embed,
    embed_m,
    embed_v,
    posit,
    posit_m,
    posit_v,
    attn_in,
    attn_in_m,
    attn_in_v,
    attn_out,
    attn_out_m,
    attn_out_v,
    mlp_in,
    mlp_in_m,
    mlp_in_v,
    mlp_out,
    mlp_out_m,
    mlp_out_v,
    small,
    small_m,
    small_v,
):
    rank = lax.axis_index("fsdp")
    length = tok_ids.shape[1]
    all_ids, all_targets, all_mask = (
        lax.all_gather(tok_ids, "fsdp", axis=0, tiled=True),
        lax.all_gather(targets, "fsdp", axis=0, tiled=True),
        lax.all_gather(loss_mask, "fsdp", axis=0, tiled=True),
    )
    all_ids = all_ids.reshape(-1)
    all_targets = all_targets.reshape(-1)
    mask_all = all_mask.reshape(-1).astype(jnp.float32)
    pos_full, w_qkv, w_out, w_up, w_down, small_full = (
        lax.all_gather(posit.astype(jnp.bfloat16), "fsdp", axis=0, tiled=True),
        lax.all_gather(attn_in.astype(jnp.bfloat16), "fsdp", axis=0, tiled=True),
        lax.all_gather(attn_out.astype(jnp.bfloat16), "fsdp", axis=0, tiled=True),
        lax.all_gather(mlp_in.astype(jnp.bfloat16), "fsdp", axis=0, tiled=True),
        lax.all_gather(mlp_out.astype(jnp.bfloat16), "fsdp", axis=0, tiled=True),
        lax.all_gather(small.astype(jnp.bfloat16), "fsdp", axis=0, tiled=True),
    )
    mats = (w_qkv, w_out, w_up, w_down)
    pieces = unpack(small_full.astype(jnp.float32))
    shard_rows = embed.shape[0]
    first_row = rank * shard_rows
    table = embed.astype(jnp.bfloat16)
    local_ids = all_ids - first_row
    inside = (local_ids >= 0) & (local_ids < shard_rows)
    safe_ids = jnp.clip(local_ids, 0, shard_rows - 1)
    looked = jnp.where(
        inside[:, None], jnp.take(table, safe_ids, axis=0), jnp.zeros((), jnp.bfloat16)
    )
    embedded = lax.psum_scatter(looked, "fsdp", scatter_dimension=0, tiled=True).astype(jnp.float32)
    inputs = embedded + pos_full[:length].astype(jnp.float32)
    final, saved = layer_forward(inputs, mats, pieces)
    final_low = final.astype(jnp.bfloat16)
    target_local = all_targets - first_row
    piece = lax.all_gather(final_low, "fsdp", axis=0, tiled=True)
    logits = dense_nt(piece, table)
    row_max = jnp.max(logits, axis=1)
    row_sum = jnp.sum(jnp.exp(logits - row_max[:, None]), axis=1)
    columns = lax.broadcasted_iota(jnp.int32, logits.shape, 1)
    row_hit = jnp.sum(jnp.where(columns == target_local[:, None], logits, 0.0), axis=1)
    maxes = row_max
    sums = row_sum
    hits = row_hit
    maxes, sums, hits = combined_all((maxes, sums, hits), "fsdp", combine_lse)
    log_total = maxes + jnp.log(sums)
    own_terms = lax.dynamic_slice_in_dim((log_total - hits) * mask_all, rank * length, length)
    loss_sum, token_total = lax.psum(
        (jnp.sum(own_terms), jnp.sum(loss_mask.astype(jnp.float32))), ("dp", "fsdp")
    )
    loss = loss_sum / token_total
    columns = lax.broadcasted_iota(jnp.int32, logits.shape, 1)
    onehot = jnp.where(columns == target_local[:, None], 1.0, 0.0)
    d_logits = (
        (jnp.exp(logits - log_total[:, None]) - onehot) * (mask_all / token_total)[:, None]
    ).astype(jnp.bfloat16)
    g_table = dense_tn(d_logits, piece)
    d_final = lax.psum_scatter(dense(d_logits, table), "fsdp", scatter_dimension=0, tiled=True)
    d_inputs, mat_grads, g_small = layer_backward(inputs, mats, pieces, saved, d_final)
    g_qkv, g_out, g_up, g_down = mat_grads
    d_low = d_inputs.astype(jnp.bfloat16)
    all_back = lax.all_gather(d_low, "fsdp", axis=0, tiled=True)
    g_table = g_table.at[safe_ids].add(
        jnp.where(inside[:, None], all_back.astype(jnp.float32), 0.0)
    )
    g_posit = jnp.concatenate(
        [d_low.astype(jnp.float32), jnp.zeros((pos_full.shape[0] - length, D), jnp.float32)], axis=0
    )
    layer_grads = (g_posit, g_qkv, g_out, g_up, g_down, g_small)
    owned = (
        lax.psum_scatter(
            layer_grads[0].astype(jnp.bfloat16), "fsdp", scatter_dimension=0, tiled=True
        ).astype(jnp.float32),
        lax.psum_scatter(
            layer_grads[1].astype(jnp.bfloat16), "fsdp", scatter_dimension=0, tiled=True
        ).astype(jnp.float32),
        lax.psum_scatter(
            layer_grads[2].astype(jnp.bfloat16), "fsdp", scatter_dimension=0, tiled=True
        ).astype(jnp.float32),
        lax.psum_scatter(
            layer_grads[3].astype(jnp.bfloat16), "fsdp", scatter_dimension=0, tiled=True
        ).astype(jnp.float32),
        lax.psum_scatter(
            layer_grads[4].astype(jnp.bfloat16), "fsdp", scatter_dimension=0, tiled=True
        ).astype(jnp.float32),
        lax.psum_scatter(
            layer_grads[5].astype(jnp.bfloat16), "fsdp", scatter_dimension=0, tiled=True
        ).astype(jnp.float32),
    )
    grads = tuple(
        lax.psum((g_table, owned[0], owned[1], owned[2], owned[3], owned[4], owned[5]), "dp")
    )
    local_sq = reduce(
        lambda acc, gradient: acc + jnp.sum(gradient * gradient), grads, jnp.float32(0.0)
    )
    grad_norm = jnp.sqrt(lax.psum(local_sq, "fsdp"))
    scale = CLIP_LIMIT / jnp.maximum(grad_norm, CLIP_LIMIT)
    params = (embed, posit, attn_in, attn_out, mlp_in, mlp_out, small)
    firsts = (embed_m, posit_m, attn_in_m, attn_out_m, mlp_in_m, mlp_out_m, small_m)
    seconds = (embed_v, posit_v, attn_in_v, attn_out_v, mlp_in_v, mlp_out_v, small_v)
    results = [loss, grad_norm]
    for weight, first_old, second_old, gradient, rate in zip(
        params, firsts, seconds, grads, rate_list()
    ):
        results.extend(adam_update(weight, first_old, second_old, gradient * scale, rate))
    return tuple(results)


def solution(mesh):
    in_specs = (
        P(("dp", "fsdp"), None),
        P(("dp", "fsdp"), None),
        P(("dp", "fsdp"), None),
        P("fsdp", None),
        P("fsdp", None),
        P("fsdp", None),
        P("fsdp", None),
        P("fsdp", None),
        P("fsdp", None),
        P("fsdp", None),
        P("fsdp", None),
        P("fsdp", None),
        P("fsdp", None),
        P("fsdp", None),
        P("fsdp", None),
        P("fsdp", None),
        P("fsdp", None),
        P("fsdp", None),
        P("fsdp", None),
        P("fsdp", None),
        P("fsdp", None),
        P("fsdp"),
        P("fsdp"),
        P("fsdp"),
    )
    out_specs = (
        P(),
        P(),
        P("fsdp", None),
        P("fsdp", None),
        P("fsdp", None),
        P("fsdp", None),
        P("fsdp", None),
        P("fsdp", None),
        P("fsdp", None),
        P("fsdp", None),
        P("fsdp", None),
        P("fsdp", None),
        P("fsdp", None),
        P("fsdp", None),
        P("fsdp", None),
        P("fsdp", None),
        P("fsdp", None),
        P("fsdp", None),
        P("fsdp", None),
        P("fsdp", None),
        P("fsdp"),
        P("fsdp"),
        P("fsdp"),
    )
    return jax.shard_map(body, mesh=mesh, in_specs=in_specs, out_specs=out_specs, check_vma=False)
```

profile of v0, /device:TPU:0, one launch (start us, length us, event | category | flops | bytes accessed | tf_op | source)
XLA Modules:
  0.0 1408.3 jit_solution(17037946089550992451)
XLA Ops:
  71.2 24.3 %all-gather.14.cloned.1.call-done = bf16[1024,768]{1,0:T(8,128)(2,1)} async-done(((bf16[128,768]{1,0:T(8,128)(2,1)}), bf16[1024,768]{1,0:T(8,128)(2,1)}) %all-gather.14.cloned.1.call-update) | async-done | bytes 1572880 | tf_op jit(solution)/shard_map/all_gather | solution.py:312
  95.5 36.8 %reduce-scatter.8.cloned.1.call-done = bf16[128,768]{1,0:T(8,128)(2,1)} async-done(((bf16[1024,768]{1,0:T(8,128)(2,1)}), bf16[128,768]{1,0:T(8,128)(2,1)}) %reduce-scatter.8.cloned.1.call-update) | async-done | bytes 196624 | tf_op jit(solution)/shard_map/reduce_scatter | solution.py:330
  134.7 39.3 %all-gather.16.cloned.1.call-done = bf16[768,2304]{1,0:T(8,128)(2,1)} async-done(((bf16[96,2304]{1,0:T(8,128)(2,1)}), bf16[768,2304]{1,0:T(8,128)(2,1)}) %all-gather.16.cloned.1.call-update) | async-done | bytes 3538960 | tf_op jit(solution)/shard_map/all_gather | solution.py:313
  180.7 17.1 %all-gather.18.cloned.1.call-done = bf16[768,768]{1,0:T(8,128)(2,1)} async-done(((bf16[96,768]{1,0:T(8,128)(2,1)}), bf16[768,768]{1,0:T(8,128)(2,1)}) %all-gather.18.cloned.1.call-update) | async-done | bytes 1179664 | tf_op jit(solution)/shard_map/all_gather | solution.py:314
  199.7 51.7 %all-gather.20.cloned.1.call-done = bf16[768,3072]{1,0:T(8,128)(2,1)} async-done(((bf16[96,3072]{1,0:T(8,128)(2,1)}), bf16[768,3072]{1,0:T(8,128)(2,1)}) %all-gather.20.cloned.1.call-update) | async-done | bytes 4718608 | tf_op jit(solution)/shard_map/all_gather | solution.py:315
  254.7 49.6 %all-gather.22.cloned.1.call-done = bf16[3072,768]{1,0:T(8,128)(2,1)} async-done(((bf16[384,768]{1,0:T(8,128)(2,1)}), bf16[3072,768]{1,0:T(8,128)(2,1)}) %all-gather.22.cloned.1.call-update) | async-done | bytes 4718608 | tf_op jit(solution)/shard_map/all_gather | solution.py:316
  334.1 18.0 %fusion.85 = (f32[1024]{0:T(1024)S(1)}, f32[1024,6288]{0,1:T(8,128)}) fusion(bf16[1024,768]{1,0:T(8,128)(2,1)} %all-gather.24.cloned.1.call-done, bf16[6288,768]{1,0:T(8,128)(2,1)} %convert_element_type.153), kind=kOutput, calls=%fused_computation.205 | convolution fusion | flops 9896606720 | bytes 36990976 | tf_op jit(solution)/shard_map/dot_general | solution.py:41
  352.1 14.0 all-gather
  378.0 14.0 all-gather.1
  392.0 14.0 all-gather.2
  407.3 39.1 %all-reduce.3 = (f32[]{:T(128)}, f32[]{:T(128)}) all-reduce(f32[]{:T(128)} %dynamic-slice_reduce_fusion, f32[]{:T(128)} %convert_reduce_fusion), channel_id=1, replica_groups=mesh['dp'=4,'fsdp'=8] {'dp','fsdp'}, use_global_device_ids=true, to_apply=%region_22.23 | all-reduce | flops 2 | bytes 16 | tf_op jit(solution)/shard_map/psum | solution.py:347
  447.1 20.3 %fusion.61 = f32[1024,768]{1,0:T(8,128)} fusion(bf16[6288,768]{1,0:T(8,128)(2,1)} %convert_element_type.153, f32[1024,6288]{0,1:T(8,128)} %get-tuple-element.172, f32[1024]{0:T(1024)S(1)} %broadcast_divide_fusion.1, f32[1024]{0:T(1024)S(1)} %get-tuple-element.134, s32[1024]{0:T(1024)S(1)} %subtract_bitcast_fusion), kind=kOutput, calls=%fused_computation.188 | convolution fusion | flops 9928802304 | bytes 38572032 | tf_op jit(solution)/shard_map/dot_general | solution.py:31
  471.9 36.1 %reduce-scatter.10.cloned.1.call-done = f32[128,768]{1,0:T(8,128)} async-done(((f32[1024,768]{1,0:T(8,128)}), f32[128,768]{1,0:T(8,128)}) %reduce-scatter.10.cloned.1.call-update) | async-done | bytes 393232 | tf_op jit(solution)/shard_map/reduce_scatter | solution.py:357
  579.5 23.1 %fusion.62 = f32[6288,768]{1,0:T(8,128)} fusion(bf16[1024,768]{1,0:T(8,128)(2,1)S(1)} %copy-done.119, f32[1024,6288]{0,1:T(8,128)} %get-tuple-element.172, f32[1024]{0:T(1024)S(1)} %copy-done.106, f32[1024]{0:T(1024)S(1)} %copy-done.108, s32[1024]{0:T(1024)S(1)} %copy-done.85), kind=kOutput, calls=%fused_computation.189 | convolution fusion | flops 9928802304 | bytes 46657536 | tf_op jit(solution)/shard_map/dot_general | solution.py:35
  602.6 22.0 %scatter_custom_fusion = f32[6288,768]{1,0:T(8,128)} fusion(f32[6288,768]{1,0:T(8,128)} %fusion.62, s32[1024]{0:T(1024)} %bitcast.146, bf16[1024,768]{1,0:T(8,128)(2,1)} %all-gather.26.cloned.1.call-done, f32[]{:T(128)} %constant.47.clone.1, pred[1024]{0:T(1024)(128)(4,1)S(1)} %copy-done.90), kind=kCustom, calls=%fused_computation.25 | custom fusion | flops 2359296 | bytes 20891136 | tf_op jit(solution)/shard_map/scatter-add | solution.py:362
  626.8 21.6 %reduce-scatter.16.cloned.1.call-done = bf16[96,768]{1,0:T(8,128)(2,1)} async-done(((bf16[768,768]{1,0:T(8,128)(2,1)}), bf16[96,768]{1,0:T(8,128)(2,1)}) %reduce-scatter.16.cloned.1.call-update) | async-done | bytes 147472 | tf_op jit(solution)/shard_map/reduce_scatter | solution.py:376
  648.4 34.6 %reduce-scatter.12.cloned.1.call-done = bf16[128,768]{1,0:T(8,128)(2,1)} async-done(((bf16[1024,768]{1,0:T(8,128)(2,1)}), bf16[128,768]{1,0:T(8,128)(2,1)}) %reduce-scatter.12.cloned.1.call-update) | async-done | bytes 196624 | tf_op jit(solution)/shard_map/reduce_scatter | solution.py:370
  682.9 44.0 %reduce-scatter.14.cloned.1.call-done = bf16[96,2304]{1,0:T(8,128)(2,1)} async-done(((bf16[768,2304]{1,0:T(8,128)(2,1)}), bf16[96,2304]{1,0:T(8,128)(2,1)}) %reduce-scatter.14.cloned.1.call-update) | async-done | bytes 442384 | tf_op jit(solution)/shard_map/reduce_scatter | solution.py:373
  727.0 56.3 %reduce-scatter.18.cloned.1.call-done = bf16[96,3072]{1,0:T(8,128)(2,1)} async-done(((bf16[768,3072]{1,0:T(8,128)(2,1)}), bf16[96,3072]{1,0:T(8,128)(2,1)}) %reduce-scatter.18.cloned.1.call-update) | async-done | bytes 589840 | tf_op jit(solution)/shard_map/reduce_scatter | solution.py:379
  783.3 56.2 %reduce-scatter.20.cloned.1.call-done = bf16[384,768]{1,0:T(8,128)(2,1)} async-done(((bf16[3072,768]{1,0:T(8,128)(2,1)}), bf16[384,768]{1,0:T(8,128)(2,1)}) %reduce-scatter.20.cloned.1.call-update) | async-done | bytes 589840 | tf_op jit(solution)/shard_map/reduce_scatter | solution.py:382
  839.5 252.9 %all-reduce.15 = (f32[128,768]{1,0:T(8,128)}, f32[96,2304]{1,0:T(8,128)S(1)}, f32[96,768]{1,0:T(8,128)S(1)}, f32[96,3072]{1,0:T(8,128)S(1)}, f32[384,768]{1,0:T(8,128)S(1)}, /*index=5*/f32[13728]{0:T(1024)}) all-reduce(bf16[128,768]{1,0:T(8,128)(2,1)} %reduce-scatter.12.cloned.1.call-done, ...), channel_id=1, replica_groups=mesh['dp'=4,'fsdp'=8] {'dp'}, use_global_device_ids=true, to_apply=%region_41.42 | all-reduce | flops 996768 | bytes 6008064 | tf_op jit(solution)/shard_map/psum | solution.py:390
  1098.8 205.0 %all-reduce.10.cloned.1.call-done = f32[6288,768]{1,0:T(8,128)} async-done(((f32[6288,768]{1,0:T(8,128)}), f32[6288,768]{1,0:T(8,128)}) %all-reduce.10.cloned.1.call-update) | async-done | bytes 19316752 | tf_op jit(solution)/shard_map/psum | solution.py:390
  1321.8 16.9 %psum.79 = f32[]{:T(128)} all-reduce(f32[]{:T(128)S(6)} %add.352), channel_id=1, replica_groups=mesh['dp'=4,'fsdp'=8] {'fsdp'}, use_global_device_ids=true, to_apply=%region_68.69 | all-reduce | flops 1 | bytes 8 | tf_op jit(solution)/shard_map/psum | solution.py:395
  1352.4 46.8 %multiply_subtract_fusion = (f32[6288,768]{1,0:T(8,128)}, f32[6288,768]{1,0:T(8,128)}, f32[6288,768]{1,0:T(8,128)}) fusion(f32[6288,768]{1,0:T(8,128)} %param.29, f32[6288,768]{1,0:T(8,128)} %all-reduce.10.cloned.1.call-done, f32[]{:T(128)S(6)} %div.286, f32[6288,768]{1,0:T(8,128)} %param.30, f32[6288,768]{1,0:T(8,128)} %param.31), kind=kLoop, calls=%fused_computation.17 | loop fusion | flops 72437760 | bytes 135217152 | tf_op jit(solution)/shard_map/sub | solution.py:261
  (453 shorter events, 229.0 us)
Async XLA Ops:
  7.2 59.3 %all-reduce.12.cloned.1.call-start = ((), (), s32[]{:S(2)}) async-start(), calls=%async_computation.22 | async-start | bytes 442368
  11.3 84.2 %all-gather.14.cloned.1.call-start = ((), (), s32[]{:S(2)}) async-start(), calls=%async_computation.8 | async-start | bytes 1769472 | tf_op jit(solution)/shard_map/all_gather | solution.py:312
  13.1 119.2 %reduce-scatter.8.cloned.1.call-start = ((), (), s32[]{:S(2)}) async-start(), calls=%async_computation.7 | async-start | bytes 1769472 | tf_op jit(solution)/shard_map/reduce_scatter | solution.py:330
  50.3 123.8 %all-gather.16.cloned.1.call-start = ((), (), s32[]{:S(2)}) async-start(), calls=%async_computation.9 | async-start | bytes 3981312 | tf_op jit(solution)/shard_map/all_gather | solution.py:313
  52.2 145.5 %all-gather.18.cloned.1.call-start = ((), (), s32[]{:S(2)}) async-start(), calls=%async_computation.10 | async-start | bytes 1327104 | tf_op jit(solution)/shard_map/all_gather | solution.py:314
  53.0 198.5 %all-gather.20.cloned.1.call-start = ((), (), s32[]{:S(2)}) async-start(), calls=%async_computation.11 | async-start | bytes 5308416 | tf_op jit(solution)/shard_map/all_gather | solution.py:315
  54.0 250.4 %all-gather.22.cloned.1.call-start = ((), (), s32[]{:S(2)}) async-start(), calls=%async_computation.12 | async-start | bytes 5308416 | tf_op jit(solution)/shard_map/all_gather | solution.py:316
  54.9 279.2 %all-gather.24.cloned.1.call-start = ((), (), s32[]{:S(2)}) async-start(), calls=%async_computation.13 | async-start | bytes 1769472 | tf_op jit(solution)/shard_map/all_gather | solution.py:335
  67.7 110.3 %copy-start.28 = (bf16[12,64,64]{2,1,0:T(8,128)(2,1)}, bf16[12,64,64]{2,1,0:T(8,128)(2,1)S(1)}, u32[]{:S(2)}) copy-start(bf16[12,64,64]{2,1,0:T(8,128)(2,1)S(1)} %convert_element_type.162) | copy-start | bytes 294916
  67.8 110.8 %copy-start.24 = (bf16[12,64,64]{2,1,0:T(8,128)(2,1)}, bf16[12,64,64]{2,1,0:T(8,128)(2,1)S(1)}, u32[]{:S(2)}) copy-start(bf16[12,64,64]{2,1,0:T(8,128)(2,1)S(1)} %convert_element_type.161) | copy-start | bytes 294916
  71.2 105.8 %copy-start.67 = (f32[768]{0:T(1024)}, f32[768]{0:T(1024)S(1)}, u32[]{:S(2)}) copy-start(f32[768]{0:T(1024)S(1)} %get-tuple-element.149) | copy-start | bytes 9220
  71.2 105.8 %copy-start.71 = (f32[768]{0:T(1024)}, f32[768]{0:T(1024)S(1)}, u32[]{:S(2)}) copy-start(f32[768]{0:T(1024)S(1)} %get-tuple-element.150) | copy-start | bytes 9220
  180.7 74.0 %copy-start.41 = (bf16[128,12,64]{0,2,1:T(8,128)(2,1)}, bf16[128,12,64]{0,2,1:T(8,128)(2,1)S(1)}, u32[]{:S(2)}) copy-start(bf16[128,12,64]{0,2,1:T(8,128)(2,1)S(1)} %get-tuple-element.165) | copy-start | bytes 589828
  310.0 198.0 %reduce-scatter.10.cloned.1.call-start = ((), (), s32[]{:S(2)}) async-start(), calls=%async_computation.14 | async-start | bytes 3538944 | tf_op jit(solution)/shard_map/reduce_scatter | solution.py:357
  329.6 117.5 %copy-start.84 = (s32[1024]{0:T(1024)}, s32[1024]{0:T(1024)S(1)}, u32[]{:S(2)}) copy-start(s32[1024]{0:T(1024)S(1)} %subtract_bitcast_fusion) | copy-start | bytes 12292
  406.7 60.8 %copy-start.107 = (f32[1024]{0:T(1024)}, f32[1024]{0:T(1024)S(1)}, u32[]{:S(2)}) copy-start(f32[1024]{0:T(1024)S(1)} %get-tuple-element.134) | copy-start | bytes 12292
  467.5 135.1 %all-gather.26.cloned.1.call-start = ((), (), s32[]{:S(2)}) async-start(), calls=%async_computation.15 | async-start | bytes 1769472 | tf_op jit(solution)/shard_map/all_gather | solution.py:361
  531.4 93.9 %all-reduce.14.cloned.1.call-start = ((), (), s32[]{:S(2)}) async-start(), calls=%async_computation.23 | async-start | bytes 442368
  559.6 88.8 %reduce-scatter.16.cloned.1.call-start = ((), (), s32[]{:S(2)}) async-start(), calls=%async_computation.19 | async-start | bytes 1327104 | tf_op jit(solution)/shard_map/reduce_scatter | solution.py:376
  562.1 120.8 %reduce-scatter.12.cloned.1.call-start = ((), (), s32[]{:S(2)}) async-start(), calls=%async_computation.17 | async-start | bytes 1769472 | tf_op jit(solution)/shard_map/reduce_scatter | solution.py:370
  564.4 162.5 %reduce-scatter.14.cloned.1.call-start = ((), (), s32[]{:S(2)}) async-start(), calls=%async_computation.18 | async-start | bytes 3981312 | tf_op jit(solution)/shard_map/reduce_scatter | solution.py:373
  568.5 214.8 %reduce-scatter.18.cloned.1.call-start = ((), (), s32[]{:S(2)}) async-start(), calls=%async_computation.20 | async-start | bytes 5308416 | tf_op jit(solution)/shard_map/reduce_scatter | solution.py:379
  573.3 266.2 %reduce-scatter.20.cloned.1.call-start = ((), (), s32[]{:S(2)}) async-start(), calls=%async_computation.21 | async-start | bytes 5308416 | tf_op jit(solution)/shard_map/reduce_scatter | solution.py:382
  578.2 725.7 %all-reduce.10.cloned.1.call-start = ((), (), s32[]{:S(2)}) async-start(), calls=%async_computation.16 | async-start | bytes 38633472 | tf_op jit(solution)/shard_map/psum | solution.py:390
  (115 other events, 837.4 us)
Sparse Core Ops, SparseCore 0:
  11.5 55.0 all-reduce.11
  68.8 26.6 all-gather.13
  98.5 33.7 reduce-scatter.7
  134.5 39.5 all-gather.15
  176.2 21.5 all-gather.17
  199.9 51.4 all-gather.19
  253.8 50.5 all-gather.21
  310.1 23.8 all-gather.23
  467.6 40.4 reduce-scatter.9
  531.5 24.2 all-gather.25
  559.7 51.3 all-reduce.13
  613.9 34.4 reduce-scatter.15
  650.7 32.2 reduce-scatter.11
  685.1 41.7 reduce-scatter.13
  729.8 53.4 reduce-scatter.17
  786.1 53.3 reduce-scatter.19
  843.9 459.9 all-reduce.9
where the time goes:
time: 1420 us; the launch traced here: 1410 us
  waiting for transfers between devices  689 us (49%)
  blocking collectives  383 us (27%)
  other arithmetic  150 us (11%)
  matrix products  105 us (7%)
  local copies, waits for them, and re-layouts  53.8 us (4%)
  between operations  26 us (2%)
    psum x1, blocking collectives, body(): lax.psum((g_table, owned[0], owned[1], owned[2], owned[3], owned[4], owne...  253 us
    psum x1, waiting for transfers between devices, body(): lax.psum((g_table, owned[0], owned[1], owned[2], owned[3], owned[4], owne...  205 us
    sub x7, other arithmetic, adam_update(): weight - rate * (first_new / bias_fix / (jnp.sqrt(second_new / bias_fix)...  58.2 us
    reduce_scatter x1, waiting for transfers between devices, body(): lax.psum_scatter(layer_grads[3].astype(jnp.bfloat16), 'fsdp', scatter_dim...  56.3 us
    reduce_scatter x1, waiting for transfers between devices, body(): lax.psum_scatter(layer_grads[4].astype(jnp.bfloat16), 'fsdp', scatter_dim...  56.2 us
    all_gather x1, waiting for transfers between devices, body(): lax.all_gather(mlp_in.astype(jnp.bfloat16), 'fsdp', axis=0, tiled=True)  51.7 us
    all_gather x1, waiting for transfers between devices, body(): lax.all_gather(mlp_out.astype(jnp.bfloat16), 'fsdp', axis=0, tiled=True)  49.6 us
    reduce_scatter x1, waiting for transfers between devices, body(): lax.psum_scatter(layer_grads[1].astype(jnp.bfloat16), 'fsdp', scatter_dim...  44 us
  transfers between devices with their start and end apart: 17, of which 15 were waited for; matrix products, arithmetic and copies ran while one was open for 10% of the time, Pallas kernels for 0%

commit v1 on v0

--- a/solution.py
+++ b/solution.py
@@ -1,8 +1,11 @@
+import functools
 from functools import reduce
 
 import jax
 import jax.numpy as jnp
 from jax import lax
+from jax.experimental import pallas as pl
+from jax.experimental.pallas import tpu as pltpu
 from jax.sharding import PartitionSpec as P
 
 D = 768
@@ -272,7 +275,7 @@
     return (top, merged, first_part[2] + second_part[2])
 
 
-def body(
+def body_general(
     tok_ids,
     targets,
     loss_mask,
@@ -405,7 +408,892 @@
     return tuple(results)
 
 
+BF = jnp.bfloat16
+F32 = jnp.float32
+MESH = pl.DeviceIdType.MESH
+TOK = 128
+GROUP = 8 * TOK
+VBLK = 1280
+
+
+def params(cid=None, mib=56):
+    if cid is None:
+        return pltpu.CompilerParams(vmem_limit_bytes=mib << 20)
+    return pltpu.CompilerParams(
+        collective_id=cid, has_side_effects=True, vmem_limit_bytes=mib << 20
+    )
+
+
+def vmem(count):
+    return [pl.BlockSpec(memory_space=pltpu.VMEM)] * count
+
+
+def sems(count):
+    return [pltpu.SemaphoreType.DMA((count,))] * 2
+
+
+class Link:
+    def __init__(self, send, recv):
+        self.send, self.recv, self.used = send, recv, 0
+
+    def copy(self, src, dst, peer, land=None):
+        slot = self.used
+        self.used += 1
+        return pltpu.make_async_remote_copy(
+            src_ref=src,
+            dst_ref=dst,
+            send_sem=self.send.at[slot],
+            recv_sem=self.recv.at[slot if land is None else land],
+            device_id=peer,
+            device_id_type=MESH,
+        )
+
+
+def greet(peers, extra=None):
+    barrier = pltpu.get_barrier_semaphore()
+    for peer in peers:
+        pl.semaphore_signal(barrier, inc=1, device_id=peer, device_id_type=MESH)
+    if extra is None:
+        pl.semaphore_wait(barrier, len(peers))
+    else:
+        flag, peer = extra
+
+        @pl.when(flag)
+        def _():
+            pl.semaphore_signal(barrier, inc=1, device_id=peer, device_id_type=MESH)
+
+        pl.semaphore_wait(barrier, len(peers) + flag.astype(jnp.int32))
+
+
+def middle_chip(fs):
+    chip = fs // 2
+    return (chip == 1) | (chip == 2)
+
+
+def ids_kernel(x_ref, o_ref, send, recv):
+    dp, fs = lax.axis_index("dp"), lax.axis_index("fsdp")
+    line = [(dp, fs ^ k) for k in range(1, 8)]
+    plane = [(dp ^ k, fs) for k in range(1, 4)]
+    greet(line + plane)
+    link = Link(send, recv)
+    o_ref[dp, fs] = x_ref[...]
+    first = [link.copy(x_ref, o_ref.at[dp, fs], peer) for peer in line]
+    for copy in first:
+        copy.start()
+    for copy in first:
+        copy.wait()
+    second = [link.copy(o_ref.at[dp], o_ref.at[dp], peer) for peer in plane]
+    for copy in second:
+        copy.start()
+    for copy in second:
+        copy.wait()
+
+
+def gather_ids(x):
+    return pl.pallas_call(
+        ids_kernel,
+        out_shape=jax.ShapeDtypeStruct((4, 8, 8, TOK), jnp.int32),
+        in_specs=vmem(1),
+        out_specs=vmem(1)[0],
+        scratch_shapes=sems(10),
+        compiler_params=params(1, 4),
+    )(x)
+
+
+class Spread:
+    slots = 8
+
+    def __init__(self, link, dp, fs, x_ref, o_ref):
+        self.fs, self.x, self.o = fs, x_ref, o_ref
+        self.mid = middle_chip(fs)
+        near, far, across, pair = [(dp, fs ^ k) for k in (2, 4, 6, 1)]
+        mine = o_ref.at[fs]
+        self.near = link.copy(x_ref, mine, near)
+        self.far = link.copy(x_ref, mine, far)
+        land = link.used
+        self.across = link.copy(x_ref, mine, across, land)
+        self.relay = link.copy(o_ref.at[fs ^ 4], o_ref.at[fs ^ 4], near, land)
+        self.pair = [
+            link.copy(x_ref if k == 0 else o_ref.at[fs ^ k], o_ref.at[fs ^ k], pair)
+            for k in (0, 2, 4, 6)
+        ]
+
+    def start(self):
+        self.far.start()
+        self.near.start()
+
+        @pl.when(self.mid)
+        def _():
+            self.across.start()
+
+        self.pair[0].start()
+        self.o[self.fs] = self.x[...]
+
+    def finish(self):
+        self.far.wait_recv()
+
+        @pl.when(self.mid)
+        def _():
+            self.relay.start()
+
+        self.pair[2].start()
+        self.near.wait_recv()
+        self.pair[1].start()
+        self.across.wait_recv()
+        self.pair[3].start()
+        for copy in self.pair:
+            copy.wait()
+        self.near.wait_send()
+        self.far.wait_send()
+
+        @pl.when(self.mid)
+        def _():
+            self.across.wait_send()
+            self.relay.wait_send()
+
+
+class Fold:
+    slots = 8
+
+    def __init__(self, link, dp, fs, x_ref, part, sums, got):
+        self.fs, self.x, self.part, self.sums, self.got = fs, x_ref, part, sums, got
+        self.mid = middle_chip(fs)
+        near, far, across, pair = [(dp, fs ^ k) for k in (2, 4, 6, 1)]
+        self.pair = [link.copy(x_ref.at[fs ^ 1 ^ (2 * k)], part.at[k], pair) for k in range(4)]
+        self.near = link.copy(sums.at[1], got.at[0], near)
+        self.far = link.copy(sums.at[2], got.at[1], far)
+        self.across = link.copy(sums.at[3], got.at[2], across)
+        self.relay = link.copy(sums.at[3], got.at[3], near)
+
+    def start(self):
+        for k in (3, 2, 1, 0):
+            self.pair[k].start()
+
+    def add(self, k):
+        self.pair[k].wait_recv()
+        return self.x[self.fs ^ (2 * k)].astype(F32) + self.part[k].astype(F32)
+
+    def middle(self):
+        self.sums[3] = self.add(3).astype(BF)
+
+        @pl.when(self.mid)
+        def _():
+            self.across.start()
+
+        @pl.when(jnp.logical_not(self.mid))
+        def _():
+            self.relay.start()
+            self.sums[2] = self.add(2).astype(BF)
+            self.far.start()
+
+        self.sums[1] = self.add(1).astype(BF)
+        self.near.start()
+
+        @pl.when(self.mid)
+        def _():
+            both = self.add(2)
+            self.relay.wait_recv()
+            self.sums[2] = (both + self.got[3].astype(F32)).astype(BF)
+            self.far.start()
+
+    def finish(self, o_ref):
+        o_ref[...] = self.add(0)
+        self.near.wait_recv()
+        o_ref[...] += self.got[0].astype(F32)
+        self.far.wait_recv()
+        o_ref[...] += self.got[1].astype(F32)
+
+        @pl.when(self.mid)
+        def _():
+            self.across.wait_recv()
+            o_ref[...] += self.got[2].astype(F32)
+            self.across.wait_send()
+
+        @pl.when(jnp.logical_not(self.mid))
+        def _():
+            self.relay.wait_send()
+
+        for copy in self.pair:
+            copy.wait_send()
+        self.near.wait_send()
+        self.far.wait_send()
+
+
+def fold_scratch():
+    return [pltpu.VMEM((4, TOK, D), BF)] * 3
+
+
+def line_peers(dp, fs):
+    return [(dp, fs ^ k) for k in (1, 2, 4)], (middle_chip(fs), (dp, fs ^ 6))
+
+
+def spread_kernel(x_ref, o_ref, send, recv):
+    dp, fs = lax.axis_index("dp"), lax.axis_index("fsdp")
+    greet(*line_peers(dp, fs))
+    spread = Spread(Link(send, recv), dp, fs, x_ref, o_ref)
+    spread.start()
+    spread.finish()
+
+
+def gather_tokens(x):
+    out = pl.pallas_call(
+        spread_kernel,
+        out_shape=jax.ShapeDtypeStruct((8, TOK, D), BF),
+        in_specs=vmem(1),
+        out_specs=vmem(1)[0],
+        scratch_shapes=sems(Spread.slots),
+        compiler_params=params(2, 16),
+    )(x)
+    return out.reshape(GROUP, D)
+
+
+def fold_kernel(x_ref, o_ref, part, sums, got, send, recv):
+    dp, fs = lax.axis_index("dp"), lax.axis_index("fsdp")
+    greet(*line_peers(dp, fs))
+    fold = Fold(Link(send, recv), dp, fs, x_ref, part, sums, got)
+    fold.start()
+    fold.middle()
+    fold.finish(o_ref)
+
+
+def sum_tokens(x):
+    return pl.pallas_call(
+        fold_kernel,
+        out_shape=jax.ShapeDtypeStruct((TOK, D), F32),
+        in_specs=vmem(1),
+        out_specs=vmem(1)[0],
+        scratch_shapes=fold_scratch() + sems(Fold.slots),
+        compiler_params=params(3, 16),
+    )(x.reshape(8, TOK, D))
+
+
+def start_kernel(
+    look, wqo, w1, small, pos, e_out, wqo_out, w1_out, small_out, pos_out, part, sums, got, send, recv
+):
+    dp, fs = lax.axis_index("dp"), lax.axis_index("fsdp")
+    core = fs % 2
+    line = [(dp, fs ^ k) for k in range(1, 8)]
+    plane = [(dp ^ k, fs) for k in range(1, 4)]
+    pair = (dp, fs ^ 1)
+    greet(line + plane)
+    link = Link(send, recv)
+    fold = Fold(link, dp, fs, look, part, sums, got)
+    fold.start()
+    high, wide = wqo.shape[0] // 2, wqo.shape[1] // 2
+    rows = pl.ds(pl.multiple_of((dp // 2) * high, 16), high)
+    cols = pl.ds(pl.multiple_of((dp % 2) * wide, 128), wide)
+    down = [
+        link.copy(wqo.at[rows, cols], wqo_out.at[fs, rows, cols], (dp, fs ^ k)) for k in (2, 4, 6)
+    ]
+    for copy in down:
+        copy.start()
+    own_pair = link.copy(wqo, wqo_out.at[fs], pair)
+    own_pair.start()
+    fold.middle()
+    tiny = [link.copy(small, small_out.at[fs], peer) for peer in line]
+    for copy in tiny:
+        copy.start()
+    width = w1_out.shape[2]
+
+    def strip(who):
+        return w1.at[:, pl.ds(pl.multiple_of(who * width, 128), width)]
+
+    strips = [link.copy(strip(fs ^ k), w1_out.at[fs], (dp, fs ^ k)) for k in range(1, 8)]
+    for copy in strips:
+        copy.start()
+    land = link.used
+    pos_line = [link.copy(pos_out, pos_out, (dp, k), land) for k in (2, 4, 6)]
+    pos_pair = link.copy(pos_out, pos_out, pair, land)
+
+    @pl.when(fs == 0)
+    def _():
+        pos_out[...] = pos[...]
+        for copy in pos_line:
+            copy.start()
+
+    wqo_out[fs] = wqo[...]
+    w1_out[fs] = strip(fs)[...]
+    small_out[fs] = small[...]
+    side = []
+    for index, k in enumerate((2, 4, 6)):
+        down[index].wait_recv()
+        piece = wqo_out.at[fs ^ k, rows, cols]
+        copies = [link.copy(piece, piece, peer) for peer in plane]
+        for copy in copies:
+            copy.start()
+        side.append(copies)
+
+    @pl.when(fs != 0)
+    def _():
+        pos_pair.wait_recv()
+
+    @pl.when(core == 0)
+    def _():
+        pos_pair.start()
+
+    fold.finish(e_out)
+    pairs = [own_pair]
+    for index, k in enumerate((2, 4, 6)):
+        for copy in side[index]:
+            copy.wait_recv()
+        copy = link.copy(wqo_out.at[fs ^ k], wqo_out.at[fs ^ k], pair)
+        copy.start()
+        pairs.append(copy)
+    for copy in tiny + strips + pairs:
+        copy.wait()
+    for copy in down + side[0] + side[1] + side[2]:
+        copy.wait_send()
+
+    @pl.when(core == 0)
+    def _():
+        pos_pair.wait_send()
+
+    @pl.when(fs == 0)
+    def _():
+        for copy in pos_line:
+            copy.wait_send()
+
+
+def start_exchange(looked, wqo, w1, small, pos):
+    n_sems = Fold.slots + 3 + 1 + 7 + 7 + 4 + 9 + 3
+    return pl.pallas_call(
+        start_kernel,
+        out_shape=(
+            jax.ShapeDtypeStruct((TOK, D), F32),
+            jax.ShapeDtypeStruct((8,) + wqo.shape, BF),
+            jax.ShapeDtypeStruct((8, w1.shape[0], w1.shape[1] // 8), BF),
+            jax.ShapeDtypeStruct((8,) + small.shape, BF),
+            jax.ShapeDtypeStruct(pos.shape, BF),
+        ),
+        in_specs=vmem(5),
+        out_specs=tuple(vmem(5)),
+        scratch_shapes=fold_scratch() + sems(n_sems),
+        compiler_params=params(4, 40),
+    )(looked.reshape(8, TOK, D), wqo, w1, small, pos)
+
+
+def lse_kernel(st_ref, o_ref, mine, got, send, recv):
+    dp, fs = lax.axis_index("dp"), lax.axis_index("fsdp")
+    line = [(dp, fs ^ k) for k in range(1, 8)]
+    plane = [(dp ^ k, fs) for k in range(1, 4)]
+    greet(line + plane)
+    link = Link(send, recv)
+    blocks = st_ref.shape[0]
+    top = st_ref[0, 0:1, :]
+    for b in range(1, blocks):
+        top = jnp.maximum(top, st_ref[b, 0:1, :])
+    total = jnp.zeros_like(top)
+    hit = jnp.zeros_like(top)
+    for b in range(blocks):
+        total = total + st_ref[b, 1:2, :] * jnp.exp(st_ref[b, 0:1, :] - top)
+        hit = hit + st_ref[b, 2:3, :]
+    for j in range(8):
+        lanes = slice(j * TOK, (j + 1) * TOK)
+        mine[j : j + 1, :] = top[:, lanes]
+        mine[8 + j : 9 + j, :] = total[:, lanes]
+        mine[16 + j : 17 + j, :] = hit[:, lanes]
+    first = [link.copy(mine, got.at[fs], peer) for peer in line]
+    for copy in first:
+        copy.start()
+    got[fs] = mine[...]
+    for copy in first:
+        copy.wait()
+    top = got[0, 0:8, :]
+    for j in range(1, 8):
+        top = jnp.maximum(top, got[j, 0:8, :])
+    total = jnp.zeros_like(top)
+    hit = jnp.zeros_like(top)
+    for j in range(8):
+        total = total + got[j, 8:16, :] * jnp.exp(got[j, 0:8, :] - top)
+        hit = hit + got[j, 16:24, :]
+    o_ref[dp, 0:8, :] = top + jnp.log(total)
+    o_ref[dp, 8:16, :] = hit
+    second = [link.copy(o_ref.at[dp], o_ref.at[dp], peer) for peer in plane]
+    for copy in second:
+        copy.start()
+    for copy in second:
+        copy.wait()
+
+
+def combine_stats(stats):
+    return pl.pallas_call(
+        lse_kernel,
+        out_shape=jax.ShapeDtypeStruct((4, 16, TOK), F32),
+        in_specs=vmem(1),
+        out_specs=vmem(1)[0],
+        scratch_shapes=[pltpu.VMEM((24, TOK), F32), pltpu.VMEM((8, 24, TOK), F32)] + sems(10),
+        compiler_params=params(5, 8),
+    )(stats)
+
+
+def total_kernel(x_ref, o_ref, got, send, recv):
+    dp, fs = lax.axis_index("dp"), lax.axis_index("fsdp")
+    line = [(dp, fs ^ k) for k in range(1, 8)]
+    greet(line)
+    link = Link(send, recv)
+    copies = [link.copy(x_ref, got.at[fs], peer) for peer in line]
+    for copy in copies:
+        copy.start()
+    got[fs] = x_ref[...]
+    for copy in copies:
+        copy.wait()
+    total = got[0]
+    for j in range(1, 8):
+        total = total + got[j]
+    o_ref[...] = total
+
+
+def line_total(x):
+    return pl.pallas_call(
+        total_kernel,
+        out_shape=jax.ShapeDtypeStruct((8, TOK), F32),
+        in_specs=vmem(1),
+        out_specs=vmem(1)[0],
+        scratch_shapes=[pltpu.VMEM((8, 8, TOK), F32)] + sems(7),
+        compiler_params=params(6, 4),
+    )(x)
+
+
+def logits_kernel(rows_here, e_ref, h_ref, t_ref, p_ref, st_ref):
+    block = pl.program_id(0)
+    logits = dense_nt(e_ref[...], h_ref[...])
+    row = lax.broadcasted_iota(jnp.int32, logits.shape, 0) + block * VBLK
+    logits = jnp.where(row < rows_here, logits, -jnp.inf)
+    top = jnp.max(logits, 0, keepdims=True)
+    st_ref[0, 2:3, :] = jnp.sum(jnp.where(row == t_ref[...], logits, 0.0), 0, keepdims=True)
+    grown = jnp.exp(logits - top)
+    st_ref[0, 0:1, :] = top
+    st_ref[0, 1:2, :] = jnp.sum(grown, 0, keepdims=True)
+    p_ref[...] = grown.astype(BF)
+
+
+def own_logits(rows_here, table, hidden, target):
+    blocks = table.shape[0] // VBLK
+    return pl.pallas_call(
+        functools.partial(logits_kernel, rows_here),
+        grid=(blocks,),
+        in_specs=[
+            pl.BlockSpec((VBLK, D), lambda i: (i, 0)),
+            pl.BlockSpec((GROUP, D), lambda i: (0, 0)),
+            pl.BlockSpec((1, GROUP), lambda i: (0, 0)),
+        ],
+        out_specs=[
+            pl.BlockSpec((VBLK, GROUP), lambda i: (i, 0)),
+            pl.BlockSpec((1, 8, GROUP), lambda i: (i, 0, 0)),
+        ],
+        out_shape=[
+            jax.ShapeDtypeStruct((table.shape[0], GROUP), BF),
+            jax.ShapeDtypeStruct((blocks, 8, GROUP), F32),
+        ],
+        compiler_params=params(),
+    )(table, hidden, target)
+
+
+def dhf_kernel(p_ref, st_ref, lse_ref, w_ref, t_ref, e_ref, o_ref, acc):
+    block = pl.program_id(0)
+    row = lax.broadcasted_iota(jnp.int32, p_ref.shape, 0) + block * VBLK
+    factor = w_ref[...] * jnp.exp(st_ref[0, 0:1, :] - lse_ref[...])
+    grad = p_ref[...].astype(F32) * factor - jnp.where(row == t_ref[...], w_ref[...], 0.0)
+    grad = grad.astype(BF)
+
+    @pl.when(block == 0)
+    def _():
+        acc[...] = dense_tn(grad, e_ref[...])
+
+    @pl.when(block > 0)
+    def _():
+        acc[...] += dense_tn(grad, e_ref[...])
+
+    @pl.when(block == pl.num_programs(0) - 1)
+    def _():
+        o_ref[...] = acc[...].astype(BF)
+
+
+def final_cotangent(grown, stats, lse, weight, target, table):
+    blocks = table.shape[0] // VBLK
+    line = pl.BlockSpec((1, GROUP), lambda i: (0, 0))
+    return pl.pallas_call(
+        dhf_kernel,
+        grid=(blocks,),
+        in_specs=[
+            pl.BlockSpec((VBLK, GROUP), lambda i: (i, 0)),
+            pl.BlockSpec((1, 8, GROUP), lambda i: (i, 0, 0)),
+            line,
+            line,
+            line,
+            pl.BlockSpec((VBLK, D), lambda i: (i, 0)),
+        ],
+        out_specs=pl.BlockSpec((GROUP, D), lambda i: (0, 0)),
+        out_shape=jax.ShapeDtypeStruct((GROUP, D), BF),
+        scratch_shapes=[pltpu.VMEM((GROUP, D), F32)],
+        compiler_params=params(),
+    )(grown, stats, lse, weight, target, table)
+
+
+def table_kernel(e_ref, h_ref, lse_ref, w_ref, t_ref, o_ref):
+    block = pl.program_id(0)
+    table = e_ref[...]
+    o_ref[...] = jnp.zeros_like(o_ref)
+
+    def group(d, carry):
+        hidden = h_ref[d]
+        logits = dense_nt(table, hidden)
+        row = lax.broadcasted_iota(jnp.int32, logits.shape, 0) + block * VBLK
+        grad = jnp.exp(logits - lse_ref[d]) * w_ref[d]
+        grad = grad - jnp.where(row == t_ref[d], w_ref[d], 0.0)
+        o_ref[...] += dense(grad.astype(BF), hidden)
+        return carry
+
+    lax.fori_loop(0, h_ref.shape[0], group, 0)
+
+
+def table_gradient(table, hidden, lse, weight, target):
+    blocks = table.shape[0] // VBLK
+    line = pl.BlockSpec((4, 1, GROUP), lambda i: (0, 0, 0))
+    return pl.pallas_call(
+        table_kernel,
+        grid=(blocks,),
+        in_specs=[
+            pl.BlockSpec((VBLK, D), lambda i: (i, 0)),
+            pl.BlockSpec((4, GROUP, D), lambda i: (0, 0, 0)),
+            line,
+            line,
+            line,
+        ],
+        out_specs=pl.BlockSpec((VBLK, D), lambda i: (i, 0)),
+        out_shape=jax.ShapeDtypeStruct((table.shape[0], D), F32),
+        compiler_params=params(),
+    )(table, hidden, lse, weight, target)
+
+
+def scatter_kernel(count_ref, list_ref, row_ref, g_hbm, d_ref, o_hbm, sq_ref, held, sem):
+    rows_here = o_hbm.shape[0]
+    load = pltpu.make_async_copy(g_hbm.at[pl.ds(0, rows_here)], held, sem.at[0])
+    load.start()
+    load.wait()
+
+    def one(i, carry):
+        token = list_ref[i]
+        row = row_ref[token]
+        held[pl.ds(row, 1), :] += d_ref[pl.ds(token, 1), :]
+        return carry
+
+    lax.fori_loop(0, count_ref[0], one, 0)
+    store = pltpu.make_async_copy(held, o_hbm, sem.at[1])
+    store.start()
+    step = 48
+
+    def square(i, carry):
+        part = held[pl.ds(pl.multiple_of(i * step, 8), step), :]
+        part = part * part
+        for j in range(step // 8):
+            carry = carry + part[j * 8 : (j + 1) * 8, :]
+        return carry
+
+    sq_ref[...] = lax.fori_loop(0, rows_here // step, square, jnp.zeros((8, D), F32))
+    store.wait()
+
+
+def add_rows(count, order, rows, gradient, d_tokens, rows_here):
+    return pl.pallas_call(
+        scatter_kernel,
+        out_shape=(
+            jax.ShapeDtypeStruct((rows_here, D), F32),
+            jax.ShapeDtypeStruct((8, D), F32),
+        ),
+        in_specs=[pl.BlockSpec(memory_space=pltpu.SMEM)] * 3
+        + [pl.BlockSpec(memory_space=pl.ANY)]
+        + vmem(1),
+        out_specs=(pl.BlockSpec(memory_space=pl.ANY), vmem(1)[0]),
+        scratch_shapes=[pltpu.VMEM((rows_here, D), F32), pltpu.SemaphoreType.DMA((2,))],
+        compiler_params=params(),
+    )(count, order, rows, gradient, d_tokens)
+
+
+def attention_forward(inputs, w_qkv, w_out, pieces):
+    gain_one, bias_one = pieces[0], pieces[1]
+    bias_qkv, bias_out, map_query, map_key = pieces[6], pieces[7], pieces[10], pieces[11]
+    length = inputs.shape[0]
+    normed_one = layer_norm(inputs, gain_one, bias_one).astype(BF)
+    project = dense(normed_one, w_qkv) + bias_qkv
+    queries = project[:, :D].astype(BF).reshape(length, H, HD)
+    keys_in = project[:, D : 2 * D].astype(BF).reshape(length, H, HD)
+    values_in = project[:, 2 * D :].astype(BF).reshape(length, H, HD)
+    maps_q = map_query.reshape(H, HD, HD).astype(BF)
+    maps_k = map_key.reshape(H, HD, HD).astype(BF)
+    inner_q = jnp.einsum("shd,hde->she", queries, maps_q, preferred_element_type=F32)
+    inner_k = jnp.einsum("shd,hde->she", keys_in, maps_k, preferred_element_type=F32)
+    feat_q = features(inner_q).astype(BF)
+    feat_k = features(inner_k).astype(BF)
+    scores = jnp.einsum("thf,shf->hts", feat_q, feat_k, preferred_element_type=F32) * causal_mask(
+        length
+    )
+    totals = jnp.sum(scores, axis=-1)
+    scores_low = scores.astype(BF)
+    numer = jnp.einsum("hts,shd->thd", scores_low, values_in, preferred_element_type=F32)
+    attended = numer / jnp.transpose(totals)[:, :, None]
+    att_low = attended.reshape(length, D).astype(BF)
+    resid_one = inputs + dense(att_low, w_out) + bias_out
+    saved = (
+        normed_one,
+        queries,
+        keys_in,
+        values_in,
+        maps_q,
+        maps_k,
+        inner_q,
+        inner_k,
+        feat_q,
+        feat_k,
+        scores_low,
+        totals,
+        numer,
+        att_low,
+    )
+    return resid_one, saved
+
+
+def attention_backward(inputs, w_qkv, w_out, pieces, saved, d_resid_one):
+    gain_one, bias_one = pieces[0], pieces[1]
+    (
+        normed_one,
+        queries,
+        keys_in,
+        values_in,
+        maps_q,
+        maps_k,
+        inner_q,
+        inner_k,
+        feat_q,
+        feat_k,
+        scores_low,
+        totals,
+        numer,
+        att_low,
+    ) = saved
+    length = inputs.shape[0]
+    d_bias_out = jnp.sum(d_resid_one, axis=0)
+    d_out_low = d_resid_one.astype(BF)
+    g_out = dense_tn(att_low, d_out_low)
+    d_attended = dense_nt(d_out_low, w_out).reshape(length, H, HD)
+    inverse = 1.0 / jnp.transpose(totals)
+    d_numer_low = (d_attended * inverse[:, :, None]).astype(BF)
+    d_totals = jnp.transpose(-jnp.sum(d_attended * numer, axis=-1) * inverse * inverse)
+    d_scores = jnp.einsum("thd,shd->hts", d_numer_low, values_in, preferred_element_type=F32)
+    d_scores_low = ((d_scores + d_totals[:, :, None]) * causal_mask(length)).astype(BF)
+    d_values = jnp.einsum("hts,thd->shd", scores_low, d_numer_low, preferred_element_type=F32)
+    d_feat_q = jnp.einsum("hts,shf->thf", d_scores_low, feat_k, preferred_element_type=F32)
+    d_feat_k = jnp.einsum("hts,thf->shf", d_scores_low, feat_q, preferred_element_type=F32)
+    unused, pull_q = jax.vjp(features, inner_q)
+    unused, pull_k = jax.vjp(features, inner_k)
+    d_inner_q = pull_q(d_feat_q)[0].astype(BF)
+    d_inner_k = pull_k(d_feat_k)[0].astype(BF)
+    g_map_q = jnp.einsum("shd,she->hde", queries, d_inner_q, preferred_element_type=F32)
+    g_map_k = jnp.einsum("shd,she->hde", keys_in, d_inner_k, preferred_element_type=F32)
+    d_queries = jnp.einsum("she,hde->shd", d_inner_q, maps_q, preferred_element_type=F32)
+    d_keys = jnp.einsum("she,hde->shd", d_inner_k, maps_k, preferred_element_type=F32)
+    d_project = jnp.concatenate(
+        [d_queries.reshape(length, D), d_keys.reshape(length, D), d_values.reshape(length, D)],
+        axis=1,
+    )
+    d_bias_qkv = jnp.sum(d_project, axis=0)
+    d_project_low = d_project.astype(BF)
+    g_qkv = dense_tn(normed_one, d_project_low)
+    d_normed_one = dense_nt(d_project_low, w_qkv)
+    d_input_part, d_gain_one, d_bias_one = norm_pull(inputs, gain_one, bias_one, d_normed_one)
+    d_inputs = d_resid_one + d_input_part
+    return d_inputs, g_qkv, g_out, (d_gain_one, d_bias_one, d_bias_qkv, d_bias_out, g_map_q, g_map_k)
+
+
+def body(
+    tok_ids,
+    targets,
+    loss_mask,
+    embed,
+    embed_m,
+    embed_v,
+    posit,
+    posit_m,
+    posit_v,
+    attn_in,
+    attn_in_m,
+    attn_in_v,
+    attn_out,
+    attn_out_m,
+    attn_out_v,
+    mlp_in,
+    mlp_in_m,
+    mlp_in_v,
+    mlp_out,
+    mlp_out_m,
+    mlp_out_v,
+    small,
+    small_m,
+    small_v,
+):
+    dp, rank = lax.axis_index("dp"), lax.axis_index("fsdp")
+    shard_rows = embed.shape[0]
+    first_row = rank * shard_rows
+    mine = jnp.concatenate([tok_ids, targets, loss_mask, jnp.zeros((5, TOK), jnp.int32)], axis=0)
+    shared = gather_ids(mine)
+    all_ids = shared[:, :, 0, :].reshape(4, GROUP)
+    all_targets = shared[:, :, 1, :].reshape(4, GROUP)
+    all_mask = shared[:, :, 2, :].reshape(4, GROUP).astype(F32)
+    token_total = jnp.sum(all_mask)
+    weight = all_mask / token_total
+    local_ids = all_ids - first_row
+    inside = (local_ids >= 0) & (local_ids < shard_rows)
+    safe_ids = jnp.clip(local_ids, 0, shard_rows - 1)
+    target_local = all_targets - first_row
+    target_here = (target_local >= 0) & (target_local < shard_rows)
+    target_local = jnp.where(target_here, target_local, -1)
+    group_ids = lax.dynamic_index_in_dim(safe_ids, dp, 0, False)
+    group_in = lax.dynamic_index_in_dim(inside, dp, 0, False)
+    own_target = lax.dynamic_slice_in_dim(target_local, dp, 1, 0)
+    own_weight = lax.dynamic_slice_in_dim(weight, dp, 1, 0)
+    looked = jnp.where(group_in[:, None], jnp.take(embed, group_ids, axis=0), 0.0).astype(BF)
+    table = jnp.pad(embed.astype(BF), ((0, -shard_rows % VBLK), (0, 0)))
+
+    small_pad = -small.shape[0] % (16 * TOK)
+    w_two = mlp_out.astype(BF)
+    embedded, wqo, w_one, small_full, positions = start_exchange(
+        looked,
+        jnp.concatenate([attn_in, attn_out], axis=1).astype(BF),
+        mlp_in.astype(BF),
+        jnp.pad(small, (0, small_pad)).astype(BF).reshape(-1, TOK),
+        posit.astype(BF),
+    )
+    wqo = wqo.reshape(D, 4 * D)
+    w_qkv, w_out = wqo[:, : 3 * D], wqo[:, 3 * D :]
+    w_one = w_one.reshape(D, FF // 8)
+    small_full = small_full.reshape(8, -1)[:, : small.shape[0]].reshape(-1)
+    pieces = unpack(small_full.astype(F32))
+    gain_two, bias_two, gain_fin, bias_fin = pieces[2:6]
+    bias_up, bias_down = pieces[8], pieces[9]
+    own_up = lax.dynamic_slice_in_dim(bias_up, rank * (FF // 8), FF // 8)
+
+    inputs = embedded + positions.astype(F32)
+    resid_one, saved = attention_forward(inputs, w_qkv, w_out, pieces)
+    normed_two = gather_tokens(layer_norm(resid_one, gain_two, bias_two).astype(BF))
+    pre_act = dense(normed_two, w_one) + own_up
+    act_low = gelu_tanh(pre_act).astype(BF)
+    resid_two = resid_one + sum_tokens(dense(act_low, w_two).astype(BF)) + bias_down
+    final = gather_tokens(layer_norm(resid_two, gain_fin, bias_fin).astype(BF))
+    all_final = lax.all_gather(final, "dp")
+
+    grown, stats = own_logits(shard_rows, table, final, own_target)
+    shared_stats = combine_stats(stats)
+    lse = shared_stats[:, :8, :].reshape(4, GROUP)
+    hits = shared_stats[:, 8:, :].reshape(4, GROUP)
+    loss = jnp.sum((lse - hits) * all_mask) / token_total
+    own_lse = lax.dynamic_slice_in_dim(lse, dp, 1, 0)
+    d_final = sum_tokens(
+        final_cotangent(grown, stats, own_lse, own_weight, own_target, table)
+    )
+
+    d_resid_two, d_gain_fin, d_bias_fin = norm_pull(resid_two, gain_fin, bias_fin, d_final)
+    d_bias_down = jnp.sum(d_resid_two, axis=0)
+    d_down_low = gather_tokens(d_resid_two.astype(BF))
+    g_down = dense_tn(act_low, d_down_low)
+    d_act = dense_nt(d_down_low, w_two)
+    unused, gelu_back = jax.vjp(gelu_tanh, pre_act)
+    d_pre = gelu_back(d_act)[0]
+    d_bias_up = lax.dynamic_update_slice_in_dim(
+        jnp.zeros((FF,), F32), jnp.sum(d_pre, axis=0), rank * (FF // 8), 0
+    )
+    d_pre_low = d_pre.astype(BF)
+    g_up = dense_tn(normed_two, d_pre_low)
+    d_normed_two = sum_tokens(dense_nt(d_pre_low, w_one).astype(BF))
+    d_resid_part, d_gain_two, d_bias_two = norm_pull(resid_one, gain_two, bias_two, d_normed_two)
+    d_resid_one = d_resid_two + d_resid_part
+    d_inputs, g_qkv, g_out, small_parts = attention_backward(
+        inputs, w_qkv, w_out, pieces, saved, d_resid_one
+    )
+    d_gain_one, d_bias_one, d_bias_qkv, d_bias_out, g_map_q, g_map_k = small_parts
+    d_low = d_inputs.astype(BF)
+    group_back = gather_tokens(d_low)
+    all_back = lax.all_gather(group_back, "dp")
+
+    g_small = jnp.concatenate(
+        [
+            d_gain_one,
+            d_bias_one,
+            d_gain_two,
+            d_bias_two,
+            d_gain_fin,
+            d_bias_fin,
+            d_bias_qkv,
+            d_bias_out,
+            d_bias_up,
+            d_bias_down,
+            g_map_q.reshape(-1),
+            g_map_k.reshape(-1),
+        ]
+    )
+    g_posit = jnp.concatenate(
+        [d_low, jnp.zeros((8 * posit.shape[0] - TOK, D), BF)], axis=0
+    )
+
+    def owned(value):
+        return lax.psum_scatter(value.astype(BF), "fsdp", scatter_dimension=0, tiled=True)
+
+    g_up_own = lax.all_to_all(
+        g_up.astype(BF).reshape(8, D // 8, FF // 8), "fsdp", 0, 0, tiled=False
+    )
+    g_up_own = jnp.transpose(g_up_own, (1, 0, 2)).reshape(D // 8, FF)
+    layer_grads = lax.psum(
+        (
+            owned(g_posit),
+            owned(g_qkv),
+            owned(g_out),
+            g_up_own,
+            g_down.astype(BF),
+            lax.psum_scatter(g_small, "fsdp", scatter_dimension=0, tiled=True),
+        ),
+        "dp",
+    )
+
+    g_table = table_gradient(
+        table,
+        all_final,
+        lse.reshape(4, 1, GROUP),
+        weight.reshape(4, 1, GROUP),
+        target_local.reshape(4, 1, GROUP),
+    )
+    flat_in = inside.reshape(-1)
+    index = lax.iota(jnp.int32, flat_in.shape[0])
+    order = lax.sort(jnp.where(flat_in, index, index + flat_in.shape[0]))
+    order = jnp.where(order < flat_in.shape[0], order, 0)
+    count = jnp.sum(flat_in.astype(jnp.int32)).reshape(1)
+    g_table, table_sq = add_rows(
+        count,
+        order,
+        safe_ids.reshape(-1),
+        g_table,
+        all_back.reshape(-1, D).astype(F32),
+        shard_rows,
+    )
+    grads = (g_table,) + tuple(g.astype(F32) for g in layer_grads)
+    local_sq = reduce(
+        lambda acc, gradient: acc + jnp.sum(gradient * gradient), grads[1:], jnp.sum(table_sq)
+    )
+    total_sq = line_total(jnp.broadcast_to(local_sq, (8, TOK)))
+    grad_norm = jnp.sqrt(total_sq[0, 0])
+    scale = CLIP_LIMIT / jnp.maximum(grad_norm, CLIP_LIMIT)
+    params_all = (embed, posit, attn_in, attn_out, mlp_in, mlp_out, small)
+    firsts = (embed_m, posit_m, attn_in_m, attn_out_m, mlp_in_m, mlp_out_m, small_m)
+    seconds = (embed_v, posit_v, attn_in_v, attn_out_v, mlp_in_v, mlp_out_v, small_v)
+    results = [loss, grad_norm]
+    for w_old, first_old, second_old, gradient, rate in zip(
+        params_all, firsts, seconds, grads, rate_list()
+    ):
+        results.extend(adam_update(w_old, first_old, second_old, gradient * scale, rate))
+    return tuple(results)
+
+
 def solution(mesh):
+    fits = mesh.shape["dp"] == 4 and mesh.shape["fsdp"] == 8
+    step = body if fits else body_general
     in_specs = (
         P(("dp", "fsdp"), None),
         P(("dp", "fsdp"), None),
@@ -457,4 +1345,4 @@
         P("fsdp"),
         P("fsdp"),
     )
-    return jax.shard_map(body, mesh=mesh, in_specs=in_specs, out_specs=out_specs, check_vma=False)
+    return jax.shard_map(step, mesh=mesh, in_specs=in_specs, out_specs=out_specs, check_vma=False)

time: 1420 us -> 922 us (0.65)
  waiting for transfers between devices: 689 us -> 275 us
  Pallas kernels: 0 us -> 381 us
  blocking collectives: 383 us -> 17.7 us
  matrix products: 105 us -> 35.2 us
  other arithmetic: 150 us -> 113 us
    pallas_call x0 -> x15, Pallas kernels: none -> 381 us  [the longest x1 97.7 us: table_gradient(): pl.pallas_call(table_kernel, grid=(blocks,), in_specs=[pl.BlockSpec((VBLK...]
    psum x3 -> x1, blocking collectives: 309 us -> 17.7 us  [body(): lax.psum((owned(g_posit), owned(g_qkv), owned(g_out), g_up_own, g_down.as...]
    reduce_scatter x7 -> x3, waiting for transfers between devices: 286 us -> 65 us  [owned(): lax.psum_scatter(value.astype(BF), 'fsdp', scatter_dimension=0, tiled=True)]
    psum x1, waiting for transfers between devices: 205 us -> 53.5 us  [body(): lax.psum((owned(g_posit), owned(g_qkv), owned(g_out), g_up_own, g_down.as...]
    all_gather x6 -> x0, blocking collectives: 74.3 us -> none  [the longest x3 42 us: combined_all(): pieces = jax.tree.map(lambda part: lax.all_gather(part, axis), value)]
    all_gather x7 -> x2, waiting for transfers between devices: 187 us -> 127 us  [the longest x1 63.9 us: body(): all_back = lax.all_gather(group_back, 'dp')]
    dot_general x5 -> x4, matrix products: 31.7 us -> 6.68 us  [dense(): return jnp.dot(left, right, preferred_element_type=jnp.float32)]
    dot_general x5 -> x4, matrix products: 36.9 us -> 12 us  [dense_tn(): lax.dot_general(left, right, (((0,), (0,)), ((), ())), preferred_element_...]
  transfers between devices with their start and end apart: 17 -> 8, of which waited for: 15 -> 6; matrix products, arithmetic and copies ran while one was open for 10% -> 8% of each run, Pallas kernels for 0% -> 2%
where the time goes in v1:
time: 922 us; the launch traced here: 914 us
  Pallas kernels  381 us (41%)
  waiting for transfers between devices  275 us (30%)
  other arithmetic  113 us (12%)
  local copies, waits for them, and re-layouts  61.9 us (7%)
  matrix products  35.2 us (4%)
  between operations  26.2 us (3%)
  blocking collectives  17.7 us (2%)
    pallas_call x1, Pallas kernels, table_gradient(): pl.pallas_call(table_kernel, grid=(blocks,), in_specs=[pl.BlockSpec((VBLK...  97.7 us
    pallas_call x4, Pallas kernels, gather_tokens(): pl.pallas_call(spread_kernel, out_shape=jax.ShapeDtypeStruct((8, TOK, D),...  78.4 us
    reduce_scatter x3, waiting for transfers between devices, owned(): lax.psum_scatter(value.astype(BF), 'fsdp', scatter_dimension=0, tiled=True)  65 us
    all_gather x1, waiting for transfers between devices, body(): all_back = lax.all_gather(group_back, 'dp')  63.9 us
    all_gather x1, waiting for transfers between devices, body(): all_final = lax.all_gather(final, 'dp')  63.5 us
    sub x7, other arithmetic, adam_update(): weight - rate * (first_new / bias_fix / (jnp.sqrt(second_new / bias_fix)...  59.6 us
    pallas_call x3, Pallas kernels, sum_tokens(): pl.pallas_call(fold_kernel, out_shape=jax.ShapeDtypeStruct((TOK, D), F32)...  54 us
    psum x1, waiting for transfers between devices, body(): lax.psum((owned(g_posit), owned(g_qkv), owned(g_out), g_up_own, g_down.as...  53.5 us
  transfers between devices with their start and end apart: 8, of which 6 were waited for; matrix products, arithmetic and copies ran while one was open for 8% of the time, Pallas kernels for 2%

profile of v1, /device:TPU:0, one launch (start us, length us, event | category | flops | bytes accessed | tf_op | source)
XLA Modules:
  0.0 914.2 jit_solution(5178703787557139492)
XLA Ops:
  7.3 11.3 %convert_element_type.161 = bf16[6288,768]{1,0:T(8,128)(2,1)} convert(f32[6288,768]{1,0:T(8,128)} %param.27) | non-fusion elementwise | flops 4829184 | bytes 28975104 | tf_op jit(solution)/shard_map/convert_element_type | solution.py:1155
  18.8 12.4 %shard_map.407 = s32[4,8,8,128]{3,2,1,0:T(8,128)S(1)} custom-call(s32[8,128]{1,0:T(8,128)S(1)} %add_add_fusion.5.x_ref), custom_call_target="tpu_custom_call" | custom-call | tf_op jit(solution)/shard_map/pallas_call | solution.py:493
  32.0 11.1 %gather_fusion = bf16[1024,768]{1,0:T(8,128)(2,1)S(1)} fusion(f32[6288,768]{1,0:T(8,128)} %param.27, s32[1024]{0:T(1024)S(1)} %broadcast_clamp_fusion.1), kind=kCustom, calls=%fused_computation | custom fusion | bytes 3149824 | tf_op jit(solution)/shard_map/jit(_take)/gather | solution.py:1154
  46.6 46.5 %shard_map.408 = (f32[128,768]{1,0:T(8,128)S(1)}, bf16[8,96,3072]{2,1,0:T(8,128)(2,1)S(1)}, bf16[8,96,384]{2,1,0:T(8,128)(2,1)S(1)}, bf16[8,112,128]{2,1,0:T(8,128)(2,1)S(1)}, bf16[128,768]{1,0:T(8,128)(2,1)S(1)}) custom-call(bf16[8,128,768]{2,1,0:T(8,128)(2,1)S(1)} %select_convert_fusion.look, bf16[96,3072]{1,0:T(8,128)(2,1)S(1)} %pad_maximum_fusion.1.wqo, ...), custom_call_target="tpu_custom_call" | custom-call | tf_op jit(solution)/shard_map/pallas_call | solution.py:759
  114.5 24.3 %shard_map.409 = bf16[8,128,768]{2,1,0:T(8,128)(2,1)S(1)} custom-call(bf16[128,768]{1,0:T(8,128)(2,1)S(1)} %add_convert_fusion.4.x_ref), custom_call_target="tpu_custom_call" | custom-call | tf_op jit(solution)/shard_map/pallas_call | solution.py:639
  142.2 18.2 %shard_map.410 = f32[128,768]{1,0:T(8,128)S(1)} custom-call(bf16[8,128,768]{2,1,0:T(8,128)(2,1)S(1)} %bitcast.155), custom_call_target="tpu_custom_call" | custom-call | tf_op jit(solution)/shard_map/pallas_call | solution.py:660
  161.5 17.9 %shard_map.411 = bf16[8,128,768]{2,1,0:T(8,128)(2,1)} custom-call(bf16[128,768]{1,0:T(8,128)(2,1)S(1)} %add_convert_fusion.3.x_ref), custom_call_target="tpu_custom_call" | custom-call | tf_op jit(solution)/shard_map/pallas_call | solution.py:639
  188.2 22.2 %shard_map.412 = (bf16[6400,1024]{1,0:T(8,128)(2,1)}, f32[5,8,1024]{2,1,0:T(8,128)}) custom-call(bf16[6400,768]{1,0:T(8,128)(2,1)} %pad.10.e_ref, bf16[1024,768]{1,0:T(8,128)(2,1)} %bitcast.17.h_ref, s32[1,1024]{1,0:T(1,128)} %and_select_fusion.1.t_ref), custom_call_target="tpu_custom_call" | custom-call | tf_op jit(solution)/shard_map/pallas_call | solution.py:872
  211.3 9.4 %shard_map.413 = f32[4,16,128]{2,1,0:T(8,128)S(1)} custom-call(f32[5,8,1024]{2,1,0:T(8,128)S(1)} %copy-done.2), custom_call_target="tpu_custom_call" | custom-call | tf_op jit(solution)/shard_map/pallas_call | solution.py:819
  223.8 22.9 %shard_map.415 = bf16[1024,768]{1,0:T(8,128)(2,1)} custom-call(bf16[6400,1024]{1,0:T(8,128)(2,1)} %get-tuple-element.41.p_ref, f32[5,8,1024]{2,1,0:T(8,128)} %get-tuple-element.39.st_ref, f32[1,1024]{1,0:T(1,128)} %get-tuple-element.140.lse_ref, f32[1,1024]{1,0:T(1,128)} %get-tuple-element.139.w_ref, s32[1,1024]{1,0:T(1,128)} %and_select_fusion.1.t_ref, ...), custom_call_target="tpu_custom_call" | custom-call | tf_op jit(solution)/shard_map/pallas_call | solution.py:915
  248.1 17.5 %shard_map.416 = f32[128,768]{1,0:T(8,128)S(1)} custom-call(bf16[8,128,768]{2,1,0:T(8,128)(2,1)S(1)} %bitcast.149), custom_call_target="tpu_custom_call" | custom-call | tf_op jit(solution)/shard_map/pallas_call | solution.py:660
  267.4 17.1 %shard_map.417 = bf16[8,128,768]{2,1,0:T(8,128)(2,1)S(1)} custom-call(bf16[128,768]{1,0:T(8,128)(2,1)S(1)} %get-tuple-element.103.x_ref), custom_call_target="tpu_custom_call" | custom-call | tf_op jit(solution)/shard_map/pallas_call | solution.py:639
  288.0 18.3 %shard_map.418 = f32[128,768]{1,0:T(8,128)S(1)} custom-call(bf16[8,128,768]{2,1,0:T(8,128)(2,1)S(1)} %bitcast.154), custom_call_target="tpu_custom_call" | custom-call | tf_op jit(solution)/shard_map/pallas_call | solution.py:660
  360.8 20.3 %reduce-scatter.4.cloned.1.call-done = bf16[128,768]{1,0:T(8,128)(2,1)} async-done(((bf16[1024,768]{1,0:T(8,128)(2,1)}), bf16[128,768]{1,0:T(8,128)(2,1)}) %reduce-scatter.4.cloned.1.call-update) | async-done | bytes 196624 | tf_op jit(solution)/shard_map/reduce_scatter | solution.py:1238
  381.1 44.7 %reduce-scatter.6.cloned.1.call-done = bf16[96,2304]{1,0:T(8,128)(2,1)} async-done(((bf16[768,2304]{1,0:T(8,128)(2,1)}), bf16[96,2304]{1,0:T(8,128)(2,1)}) %reduce-scatter.6.cloned.1.call-update) | async-done | bytes 442384 | tf_op jit(solution)/shard_map/reduce_scatter | solution.py:1238
  425.9 19.2 %shard_map.419 = bf16[8,128,768]{2,1,0:T(8,128)(2,1)} custom-call(bf16[128,768]{1,0:T(8,128)(2,1)S(1)} %add_convert_fusion.x_ref), custom_call_target="tpu_custom_call" | custom-call | tf_op jit(solution)/shard_map/pallas_call | solution.py:639
  456.6 27.9 %all-reduce.8.cloned.1.call-done = f32[109824]{0:T(1024)} async-done(((f32[109824]{0:T(1024)}), f32[109824]{0:T(1024)}) %all-reduce.8.cloned.1.call-update) | async-done | bytes 439312
  485.4 17.7 %psum.47 = f32[13728]{0:T(1024)S(1)} all-reduce(f32[13728]{0:T(1024)S(1)} %dynamic-slice.1), channel_id=1, replica_groups=mesh['dp'=4,'fsdp'=8] {'dp'}, use_global_device_ids=true, to_apply=%region_55.56 | all-reduce | flops 13728 | bytes 109824 | tf_op jit(solution)/shard_map/psum | solution.py:1244
  503.7 53.5 %all-reduce.10.cloned.1.call-done = (bf16[128,768]{1,0:T(8,128)(2,1)}, bf16[96,2304]{1,0:T(8,128)(2,1)}, bf16[96,768]{1,0:T(8,128)(2,1)}, bf16[96,3072]{1,0:T(8,128)(2,1)}, bf16[384,768]{1,0:T(8,128)(2,1)}) async-done(((bf16[128,768]{1,0:T(8,128)(2,1)}, bf16[96,2304]{1,0:T(8,128)(2,1)}, bf16[96,768]{1,0:T(8,128)(2,1)}, bf16[96,3072]{1,0:T(8,128)(2,1)}, bf16[384,768]{1,0:T(8,128)(2,1)}), ...) | async-done | bytes 1966096 | tf_op jit(solution)/shard_map/psum | solution.py:1244
  565.2 63.9 %all-gather.5.cloned.1.call-done = bf16[4,1024,768]{2,1,0:T(8,128)(2,1)} async-done(((bf16[1,1024,768]{2,1,0:T(8,128)(2,1)}), bf16[4,1024,768]{2,1,0:T(8,128)(2,1)}) %all-gather.5.cloned.1.call-update) | async-done | bytes 6291472 | tf_op jit(solution)/shard_map/all_gather | solution.py:1215
  637.6 63.5 %all-gather.3.cloned.1.call-done.h_ref = bf16[4,1024,768]{2,1,0:T(8,128)(2,1)} async-done(((bf16[1,1024,768]{2,1,0:T(8,128)(2,1)}), bf16[4,1024,768]{2,1,0:T(8,128)(2,1)}) %all-gather.3.cloned.1.call-update) | async-done | bytes 6291472 | tf_op jit(solution)/shard_map/all_gather | solution.py:1182
  701.1 97.7 %shard_map.414.g_hbm = f32[6400,768]{1,0:T(8,128)} custom-call(bf16[6400,768]{1,0:T(8,128)(2,1)} %pad.10.e_ref, bf16[4,1024,768]{2,1,0:T(8,128)(2,1)} %all-gather.3.cloned.1.call-done.h_ref, f32[4,1,1024]{2,1,0:T(1,128)} %bitcast.197, f32[4,1,1024]{2,1,0:T(1,128)} %bitcast.198, s32[4,1,1024]{2,1,0:T(1,128)} %and_select_fusion.t_ref), custom_call_target="tpu_custom_call" | custom-call | tf_op jit(solution)/shard_map/pallas_call | solution.py:953
  798.8 31.8 %shard_map.420 = (f32[6288,768]{1,0:T(8,128)}, f32[8,768]{1,0:T(8,128)}) custom-call(s32[1]{0:T(128)} %bitcast.19.count_ref, s32[4096]{0:T(1024)} %compare_select_fusion.list_ref, s32[4096]{0:T(1024)} %bitcast.196, f32[6400,768]{1,0:T(8,128)} %shard_map.414.g_hbm, f32[4096,768]{1,0:T(8,128)} %bitcast_convert_fusion.d_ref), custom_call_target="tpu_custom_call" | custom-call | tf_op jit(solution)/shard_map/pallas_call | solution.py:998
  857.9 46.8 %multiply_subtract_fusion = (f32[6288,768]{1,0:T(8,128)}, f32[6288,768]{1,0:T(8,128)}, f32[6288,768]{1,0:T(8,128)}) fusion(f32[6288,768]{1,0:T(8,128)} %param.27, f32[6288,768]{1,0:T(8,128)} %get-tuple-element.43, f32[]{:T(128)S(6)} %div.297, f32[6288,768]{1,0:T(8,128)} %param.28, f32[6288,768]{1,0:T(8,128)} %param.29), kind=kLoop, calls=%fused_computation.8 | loop fusion | flops 72437760 | bytes 135217152 | tf_op jit(solution)/shard_map/sub | solution.py:264
  (462 shorter events, 152.1 us)
Async XLA Ops:
  7.2 353.6 %reduce-scatter.8.cloned.1.call-start = ((), (), s32[]{:S(2)}) async-start(), calls=%async_computation.8 | async-start | bytes 1327104 | tf_op jit(solution)/shard_map/reduce_scatter | solution.py:1238
  96.0 43.6 %copy-start.7 = (bf16[8,96,384]{2,1,0:T(8,128)(2,1)}, bf16[8,96,384]{2,1,0:T(8,128)(2,1)S(1)}, u32[]{:S(2)}) copy-start(bf16[8,96,384]{2,1,0:T(8,128)(2,1)S(1)} %get-tuple-element.38) | copy-start | bytes 1769476
  114.1 25.5 %copy-start.9 = (f32[128,768]{1,0:T(8,128)}, f32[128,768]{1,0:T(8,128)S(1)}, u32[]{:S(2)}) copy-start(f32[128,768]{1,0:T(8,128)S(1)} %get-tuple-element.135) | copy-start | bytes 1179652
  114.1 26.5 %copy-start.114 = (f32[128]{0:T(128)}, f32[128]{0:T(128)S(1)}, u32[]{:S(2)}) copy-start(f32[128]{0:T(128)S(1)} %broadcast_multiply_fusion.1) | copy-start | bytes 1540
  114.3 24.5 %copy-start.130 = (f32[128]{0:T(128)}, f32[128]{0:T(128)S(1)}, u32[]{:S(2)}) copy-start(f32[128]{0:T(128)S(1)} %multiply_reduce_fusion.12) | copy-start | bytes 1540
  114.3 26.3 %copy-start.120 = (f32[128]{0:T(128)}, f32[128]{0:T(128)S(1)}, u32[]{:S(2)}) copy-start(f32[128]{0:T(128)S(1)} %fusion.60) | copy-start | bytes 1540
  142.1 19.2 %copy-start.91 = (f32[768]{0:T(1024)S(1)}, f32[768]{0:T(1024)}, u32[]{:S(2)}) copy-start(f32[768]{0:T(1024)} %get-tuple-element.104) | copy-start | bytes 9220
  142.2 19.2 %copy-start.102 = (f32[768]{0:T(1024)S(1)}, f32[768]{0:T(1024)}, u32[]{:S(2)}) copy-start(f32[768]{0:T(1024)} %get-tuple-element.105) | copy-start | bytes 9220
  160.5 18.8 %copy-start.93 = (s32[4,8,128]{2,1,0:T(8,128)S(1)}, s32[4,8,128]{2,1,0:T(8,128)}, u32[]{:S(2)}) copy-start(s32[4,8,128]{2,1,0:T(8,128)} %get-tuple-element.114) | copy-start | bytes 49156
  246.7 18.9 %copy-start.117 = (f32[128]{0:T(128)S(1)}, f32[128]{0:T(128)}, u32[]{:S(2)}) copy-start(f32[128]{0:T(128)} %copy-done.116) | copy-start | bytes 1540
  246.7 19.0 %copy-start.123 = (f32[128]{0:T(128)S(1)}, f32[128]{0:T(128)}, u32[]{:S(2)}) copy-start(f32[128]{0:T(128)} %copy-done.122) | copy-start | bytes 1540
  246.7 19.7 %copy-start.133 = (f32[128]{0:T(128)S(1)}, f32[128]{0:T(128)}, u32[]{:S(2)}) copy-start(f32[128]{0:T(128)} %copy-done.132) | copy-start | bytes 1540
  286.9 19.4 %copy-start.138 = (bf16[1024,384]{1,0:T(8,128)(2,1)}, bf16[1024,384]{1,0:T(8,128)(2,1)S(1)}, u32[]{:S(2)}) copy-start(bf16[1024,384]{1,0:T(8,128)(2,1)S(1)} %get-tuple-element.138) | copy-start | bytes 2359300
  288.0 19.1 %copy-start.131 = (f32[128]{0:T(128)S(1)}, f32[128]{0:T(128)}, u32[]{:S(2)}) copy-start(f32[128]{0:T(128)} %copy-done.130) | copy-start | bytes 1540
  310.4 70.7 %reduce-scatter.4.cloned.1.call-start = ((), (), s32[]{:S(2)}) async-start(), calls=%async_computation.6 | async-start | bytes 1769472 | tf_op jit(solution)/shard_map/reduce_scatter | solution.py:1238
  320.4 105.4 %reduce-scatter.6.cloned.1.call-start = ((), (), s32[]{:S(2)}) async-start(), calls=%async_computation.7 | async-start | bytes 3981312 | tf_op jit(solution)/shard_map/reduce_scatter | solution.py:1238
  327.8 31.0 %all-to-all-start = ((bf16[8,96,384]{2,1,0:T(8,128)(2,1)}), bf16[8,96,384]{2,1,0:T(8,128)(2,1)}, u32[]{:S(2)}, u32[]{:S(2)}) async-start(bf16[8,96,384]{2,1,0:T(8,128)(2,1)} %bitcast.190), calls=%async_computation.3 | async-start | bytes 1179648 | tf_op jit(solution)/shard_map/all_to_all | solution.py:1240
  332.2 152.3 %all-reduce.8.cloned.1.call-start = ((), (), s32[]{:S(2)}) async-start(), calls=%async_computation.9 | async-start | bytes 884736
  355.4 201.8 %all-reduce.10.cloned.1.call-start = ((), (), s32[]{:S(2)}) async-start(), calls=%async_computation.10 | async-start | bytes 3932160 | tf_op jit(solution)/shard_map/psum | solution.py:1244
  425.8 203.2 %all-gather.5.cloned.1.call-start = ((), (), s32[]{:S(2)}) async-start(), calls=%async_computation.5 | async-start | bytes 7864320 | tf_op jit(solution)/shard_map/all_gather | solution.py:1215
  445.1 256.0 %all-gather.3.cloned.1.call-start = ((), (), s32[]{:S(2)}) async-start(), calls=%async_computation.4 | async-start | bytes 7864320 | tf_op jit(solution)/shard_map/all_gather | solution.py:1182
  798.8 44.9 %copy-start.49 = (f32[128,768]{1,0:T(8,128)S(1)}, f32[128,768]{1,0:T(8,128)}, u32[]{:S(2)}) copy-start(f32[128,768]{1,0:T(8,128)} %param.30) | copy-start | bytes 1179652
  798.8 44.9 %copy-start.73 = (bf16[128,768]{1,0:T(8,128)(2,1)S(1)}, bf16[128,768]{1,0:T(8,128)(2,1)}, u32[]{:S(2)}) copy-start(bf16[128,768]{1,0:T(8,128)(2,1)} %get-tuple-element.57) | copy-start | bytes 589828
  798.8 44.9 %copy-start.78 = (f32[128,768]{1,0:T(8,128)S(1)}, f32[128,768]{1,0:T(8,128)}, u32[]{:S(2)}) copy-start(f32[128,768]{1,0:T(8,128)} %param.31) | copy-start | bytes 1179652
  (127 other events, 640.0 us)
Sparse Core Ops, SparseCore 0:
  310.5 33.8 reduce-scatter.7
  347.2 33.8 reduce-scatter.3
  384.0 41.7 reduce-scatter.5
  428.7 55.7 all-reduce.7
  488.6 68.5 all-reduce.9
  558.9 70.1 all-gather.4
  630.9 70.1 all-gather.2
